TPU v7x, 256 devices: a whole 4x4x8 slice. The times are simulated.
256 devices in a mesh: seq: 32 (over x, z_lo, y), dp: 8 (over z_hi, core).
Axes of the slice: x: 4, y: 4, z: 8 (z_hi: 4, z_lo: 2; z = z_hi * 2 + z_lo), core: 2. Of those that a mesh axis runs over, the one named last changes fastest.
Arguments:
- normed_input: bfloat16 [8, 4096, 5120], P('dp', 'seq'), may hold values from -6 to 6
- query_states: bfloat16 [8, 4096, 4096], P('dp', 'seq'), may hold values from -6 to 6
- rotated_key_states: bfloat16 [8, 4096, 512], P('dp', 'seq'), may hold values from -6 to 6
- value_state_rows: bfloat16 [8, 4096, 512], P('dp', 'seq'), may hold values from -6 to 6
- attn_output: bfloat16 [8, 4096, 4096], P('dp', 'seq'), may hold values from -6 to 6
- output_grad: bfloat16 [8, 4096, 4096], P('dp', 'seq'), may hold values from -6 to 6
Outputs:
- query_grad: bfloat16 [8, 4096, 4096], P('dp', 'seq')
- key_gradient: bfloat16 [8, 4096, 512], P('dp', 'seq')
- value_gradient: bfloat16 [8, 4096, 512], P('dp', 'seq')
- weight_grad: float32 [5120, 512], P(('seq', 'dp'))
All inputs are finite; a program needn't handle non-finite values.
Results may differ from a plain program's by a relative error of at most 0.012.
Values may be sent and summed in bfloat16 or wider, within the bound.
A program may use at most 128 MiB of HBM per device.

v0:
```python
import jax
import jax.numpy as jnp
from jax import lax
from jax.sharding import PartitionSpec as P

QUERY_HEADS = 32
KEY_VALUE_HEADS = 4
HEAD_SIZE = 128


def attend_backward(query_heads, pair_full, output_heads, grad_heads):
    seq_length, heads_dev, head_dim = query_heads.shape
    key_full = pair_full[:, :head_dim]
    value_full = pair_full[:, head_dim:]
    score_scale = head_dim ** (-0.5)
    block_rows = min(512, seq_length)
    block_count = seq_length // block_rows
    row_delta = jnp.sum(grad_heads.astype(jnp.float32) * output_heads.astype(jnp.float32), axis=2)
    key_blocks = [
        jnp.zeros((block_rows, head_dim), jnp.float32) for block_index in range(block_count)
    ]
    value_blocks = [
        jnp.zeros((block_rows, head_dim), jnp.float32) for block_index in range(block_count)
    ]
    query_blocks = []
    for row_block in range(block_count):
        first_query = row_block * block_rows
        end_query = first_query + block_rows
        query_rows = query_heads[first_query:end_query]
        grad_rows = grad_heads[first_query:end_query]
        key_rows = key_full[:end_query]
        value_rows = value_full[:end_query]
        scores = (
            jnp.einsum("qhd,kd->hqk", query_rows, key_rows, preferred_element_type=jnp.float32)
            * score_scale
        )
        query_index = first_query + jnp.arange(block_rows, dtype=jnp.int32)
        key_index = jnp.arange(end_query, dtype=jnp.int32)
        visible = key_index[None, :] <= query_index[:, None]
        scores = jnp.where(visible[None], scores, -jnp.inf)
        row_max = jnp.max(scores, axis=2, keepdims=True)
        row_total = jnp.sum(jnp.exp(scores - row_max), axis=2, keepdims=True)
        prob_grads = jnp.einsum(
            "qhd,kd->hqk", grad_rows, value_rows, preferred_element_type=jnp.float32
        )
        weights = jnp.exp(scores - row_max) / row_total
        weights_low = weights.astype(jnp.bfloat16)
        delta_rows = row_delta[first_query:end_query].T[:, :, None]
        score_grads = (weights * (prob_grads - delta_rows) * score_scale).astype(jnp.bfloat16)
        value_partial = jnp.einsum(
            "hqk,qhd->kd", weights_low, grad_rows, preferred_element_type=jnp.float32
        )
        query_blocks.append(
            jnp.einsum(
                "hqk,kd->qhd", score_grads, key_rows, preferred_element_type=jnp.float32
            ).astype(jnp.bfloat16)
        )
        key_partial = jnp.einsum(
            "hqk,qhd->kd", score_grads, query_rows, preferred_element_type=jnp.float32
        )
        for key_block in range(row_block + 1):
            low_row = key_block * block_rows
            key_blocks[key_block] = (
                key_blocks[key_block] + key_partial[low_row : low_row + block_rows]
            )
            value_blocks[key_block] = (
                value_blocks[key_block] + value_partial[low_row : low_row + block_rows]
            )
    key_total = jnp.concatenate(key_blocks, axis=0)
    value_total = jnp.concatenate(value_blocks, axis=0)
    return (jnp.concatenate(query_blocks, axis=0), key_total, value_total)


def per_device(
    normed_input, query_states, rotated_key_states, value_state_rows, attn_output, output_grad
):
    sequence_workers = lax.axis_size("seq")
    token_rows = query_states.shape[1]
    seq_length = token_rows * sequence_workers
    heads_dev = QUERY_HEADS // sequence_workers
    sharer_group = sequence_workers // KEY_VALUE_HEADS
    head_width = heads_dev * HEAD_SIZE
    query_send = query_states.reshape(token_rows, sequence_workers, head_width)
    output_send = attn_output.reshape(token_rows, sequence_workers, head_width)
    grad_send = output_grad.reshape(token_rows, sequence_workers, head_width)
    key_value = jnp.concatenate(
        [
            rotated_key_states.reshape(token_rows, KEY_VALUE_HEADS, HEAD_SIZE),
            value_state_rows.reshape(token_rows, KEY_VALUE_HEADS, HEAD_SIZE),
        ],
        axis=2,
    )
    pair_outbound = jnp.repeat(key_value, sharer_group, axis=1)
    query_arrived, output_arrived, grad_arrived, pair_arrived = (
        lax.all_to_all(query_send, "seq", split_axis=1, concat_axis=0, tiled=True),
        lax.all_to_all(output_send, "seq", split_axis=1, concat_axis=0, tiled=True),
        lax.all_to_all(grad_send, "seq", split_axis=1, concat_axis=0, tiled=True),
        lax.all_to_all(pair_outbound, "seq", split_axis=1, concat_axis=0, tiled=True),
    )
    pair_full = pair_arrived.reshape(seq_length, 2 * HEAD_SIZE)
    query_grads, key_total, value_total = attend_backward(
        query_arrived, pair_full, output_arrived, grad_arrived
    )
    query_back = lax.all_to_all(
        query_grads.reshape(sequence_workers, token_rows, head_width),
        "seq",
        split_axis=0,
        concat_axis=0,
        tiled=True,
    )
    query_grad = query_back.transpose(1, 0, 2).reshape(1, token_rows, QUERY_HEADS * HEAD_SIZE)
    partial_value = jnp.concatenate([key_total, value_total], axis=1)
    pair_returned = lax.all_to_all(
        partial_value.reshape(sequence_workers, token_rows, 2 * HEAD_SIZE).astype(jnp.bfloat16),
        "seq",
        split_axis=0,
        concat_axis=0,
        tiled=True,
    ).astype(jnp.float32)
    pair_gradients = (
        pair_returned.reshape(KEY_VALUE_HEADS, sharer_group, token_rows, 2 * HEAD_SIZE)
        .sum(axis=1)
        .transpose(1, 0, 2)
    )
    pair_lower = pair_gradients.astype(jnp.bfloat16)
    key_gradient = pair_lower[:, :, :HEAD_SIZE].reshape(1, token_rows, KEY_VALUE_HEADS * HEAD_SIZE)
    value_lower = pair_lower[:, :, HEAD_SIZE:].reshape(token_rows, KEY_VALUE_HEADS * HEAD_SIZE)
    value_gradient = value_lower.reshape(1, token_rows, KEY_VALUE_HEADS * HEAD_SIZE)
    input_rows = normed_input.reshape(token_rows, normed_input.shape[2])
    weight_grad = lax.psum_scatter(
        jnp.einsum("td,tc->dc", input_rows, value_lower, preferred_element_type=jnp.float32),
        ("seq", "dp"),
        scatter_dimension=0,
        tiled=True,
    )
    return (query_grad, key_gradient, value_gradient, weight_grad)


def solution(mesh):
    placed = (
        P("dp", "seq", None),
        P("dp", "seq", None),
        P("dp", "seq", None),
        P("dp", "seq", None),
        P("dp", "seq", None),
        P("dp", "seq", None),
    )
    return jax.shard_map(
        per_device,
        mesh=mesh,
        in_specs=placed,
        out_specs=(
            P("dp", "seq", None),
            P("dp", "seq", None),
            P("dp", "seq", None),
            P(("seq", "dp"), None),
        ),
        check_vma=False,
    )
```

profile of v0, /device:TPU:6, one launch (start us, length us, event | category | flops | bytes accessed | tf_op | source)
XLA Modules:
  0.0 502.7 jit_solution(5944545456067562414)
XLA Ops:
  7.2 2.4 copy.61
  9.6 9.0 %all-to-all-start.1 = ((bf16[128,32,128]{0,2,1:T(8,128)(2,1)}), bf16[128,32,128]{0,2,1:T(8,128)(2,1)S(1)}, u32[]{:S(2)}, u32[]{:S(2)}) async-start(bf16[128,32,128]{0,2,1:T(8,128)(2,1)} %bitcast.4), calls=%async_computation.1 | async-start | bytes 2097152 | tf_op jit(solution)/shard_map/all_to_all | solution.py:95
  18.6 1.3 copy.65
  19.9 13.5 %all-to-all-done.1 = bf16[128,32,128]{0,2,1:T(8,128)(2,1)S(1)} async-done(((bf16[128,32,128]{0,2,1:T(8,128)(2,1)}), bf16[128,32,128]{0,2,1:T(8,128)(2,1)S(1)}, u32[]{:S(2)}, u32[]{:S(2)}) %all-to-all-start.1) | async-done | bytes 1048608 | tf_op jit(solution)/shard_map/all_to_all | solution.py:95
  33.4 6.6 %all-to-all-start.3 = ((bf16[128,32,128]{0,2,1:T(8,128)(2,1)}), bf16[128,32,128]{0,2,1:T(8,128)(2,1)}, u32[]{:S(2)}, u32[]{:S(2)}) async-start(bf16[128,32,128]{0,2,1:T(8,128)(2,1)} %bitcast.18), calls=%async_computation.3 | async-start | bytes 2097152 | tf_op jit(solution)/shard_map/all_to_all | solution.py:96
  40.0 2.3 copy.63
  42.3 11.5 %all-to-all-done.3 = bf16[128,32,128]{0,2,1:T(8,128)(2,1)} async-done(((bf16[128,32,128]{0,2,1:T(8,128)(2,1)}), bf16[128,32,128]{0,2,1:T(8,128)(2,1)}, u32[]{:S(2)}, u32[]{:S(2)}) %all-to-all-start.3) | async-done | bytes 1048608 | tf_op jit(solution)/shard_map/all_to_all | solution.py:96
  53.9 6.3 %all-to-all-start.2 = ((bf16[128,32,128]{0,2,1:T(8,128)(2,1)}), bf16[128,32,128]{0,2,1:T(8,128)(2,1)S(1)}, u32[]{:S(2)}, u32[]{:S(2)}) async-start(bf16[128,32,128]{0,2,1:T(8,128)(2,1)} %bitcast.12), calls=%async_computation.2 | async-start | bytes 2097152 | tf_op jit(solution)/shard_map/all_to_all | solution.py:97
  60.4 12.7 %all-to-all-done.2 = bf16[128,32,128]{0,2,1:T(8,128)(2,1)S(1)} async-done(((bf16[128,32,128]{0,2,1:T(8,128)(2,1)}), bf16[128,32,128]{0,2,1:T(8,128)(2,1)S(1)}, u32[]{:S(2)}, u32[]{:S(2)}) %all-to-all-start.2) | async-done | bytes 1048608 | tf_op jit(solution)/shard_map/all_to_all | solution.py:97
  73.2 1.7 broadcast_in_dim.30
  74.9 6.3 %all-to-all-start = ((bf16[128,32,256]{2,0,1:T(8,128)(2,1)}), bf16[128,32,256]{2,0,1:T(8,128)(2,1)S(1)}, u32[]{:S(2)}, u32[]{:S(2)}) async-start(bf16[128,32,256]{2,0,1:T(8,128)(2,1)} %bitcast.409), calls=%async_computation | async-start | bytes 4194304 | tf_op jit(solution)/shard_map/all_to_all | solution.py:98
  85.6 2.2 fusion.166
  88.8 1.7 copy.76
  90.5 1.7 copy.74
  92.2 1.7 copy.72
  93.8 1.7 copy.70
  95.5 1.7 copy.68
  97.2 1.7 copy.66
  98.8 1.7 copy.62
  100.5 2.2 fusion.167
  102.7 1.7 copy.79
  104.4 1.7 copy.77
  106.0 1.7 copy.75
  107.7 1.6 copy.73
  109.3 1.7 copy.71
  111.0 1.7 copy.69
  112.7 1.7 copy.67
  114.3 1.7 copy.64
  116.0 1.9 fusion.50
  119.8 1.4 fusion.170
  126.0 1.5 fusion.59
  133.8 1.4 fusion.173
  137.2 1.5 fusion.23
  143.3 2.1 fusion.24
  150.6 2.2 fusion.12
  154.6 1.4 fusion.176
  157.1 1.5 fusion.18
  158.6 3.4 fusion.13
  167.8 32.0 %all_to_all.64 = bf16[32,128,256]{2,1,0:T(8,128)(2,1)S(1)} all-to-all(bf16[32,128,256]{2,1,0:T(8,128)(2,1)S(1)} %bitcast.410), channel_id=1, replica_groups=mesh['seq'=32,'dp'=8] {'seq'}, dimensions={0} | all-to-all | bytes 4194304 | tf_op jit(solution)/shard_map/all_to_all | solution.py:113
  201.9 5.4 %convolution_bitcast_fusion = f32[5120,512]{0,1:T(8,128)} fusion(bf16[128,512]{0,1:T(8,128)(2,1)S(1)} %bitcast.415, bf16[1,128,5120]{2,1,0:T(8,128)(2,1)S(1)} %copy-done), kind=kOutput, calls=%fused_computation.7 | convolution fusion | flops 671088640 | bytes 11927552 | tf_op jit(solution)/shard_map/td,tc->dc/dot_general | solution.py:131
  207.3 1.4 fusion.91
  208.7 1.7 fusion.99
  210.4 1.8 fusion.103
  216.0 1.5 copy-done.4
  218.6 1.4 copy.80
  219.9 6.4 %all-to-all-start.4 = ((bf16[32,128,128]{1,2,0:T(8,128)(2,1)}), bf16[32,128,128]{1,2,0:T(8,128)(2,1)S(1)}, u32[]{:S(2)}, u32[]{:S(2)}) async-start(bf16[32,128,128]{1,2,0:T(8,128)(2,1)} %copy.80), calls=%async_computation.4 | async-start | bytes 2097152 | tf_op jit(solution)/shard_map/all_to_all | solution.py:104
  226.3 18.2 %all-to-all-done.4 = bf16[32,128,128]{1,2,0:T(8,128)(2,1)S(1)} async-done(((bf16[32,128,128]{1,2,0:T(8,128)(2,1)}), bf16[32,128,128]{1,2,0:T(8,128)(2,1)S(1)}, u32[]{:S(2)}, u32[]{:S(2)}) %all-to-all-start.4) | async-done | bytes 1048608 | tf_op jit(solution)/shard_map/all_to_all | solution.py:104
  247.5 246.2 %all-reduce.3.cloned.1.call-done = f32[5120,512]{0,1:T(8,128)} async-done(((f32[5120,512]{0,1:T(8,128)}), f32[5120,512]{0,1:T(8,128)}) %all-reduce.3.cloned.1.call-update) | async-done | bytes 10485776
  (177 shorter events, 50.6 us)
Async XLA Ops:
  7.2 194.7 %copy-start = (bf16[1,128,5120]{2,1,0:T(8,128)(2,1)S(1)}, bf16[1,128,5120]{2,1,0:T(8,128)(2,1)}, u32[]{:S(2)}) copy-start(bf16[1,128,5120]{2,1,0:T(8,128)(2,1)} %param.6) | copy-start | bytes 3932164
  7.2 11.4 %copy-start.16 = (bf16[1,128,4096]{2,1,0:T(8,128)(2,1)S(1)}, bf16[1,128,4096]{2,1,0:T(8,128)(2,1)}, u32[]{:S(2)}) copy-start(bf16[1,128,4096]{2,1,0:T(8,128)(2,1)} %param.10) | copy-start | bytes 3145732
  9.6 23.8 %all-to-all-start.1 = ((bf16[128,32,128]{0,2,1:T(8,128)(2,1)}), bf16[128,32,128]{0,2,1:T(8,128)(2,1)S(1)}, u32[]{:S(2)}, u32[]{:S(2)}) async-start(bf16[128,32,128]{0,2,1:T(8,128)(2,1)} %bitcast.4), calls=%async_computation.1 | async-start | bytes 2097152 | tf_op jit(solution)/shard_map/all_to_all | solution.py:95
  33.4 20.4 %copy-start.13 = (bf16[128,32,128]{0,2,1:T(8,128)(2,1)}, bf16[128,32,128]{0,2,1:T(8,128)(2,1)S(1)}, u32[]{:S(2)}) copy-start(bf16[128,32,128]{0,2,1:T(8,128)(2,1)S(1)} %all-to-all-done.1) | copy-start | bytes 3145732
  33.4 26.7 %copy-start.27 = (bf16[1,128,512]{2,1,0:T(8,128)(2,1)S(1)}, bf16[1,128,512]{2,1,0:T(8,128)(2,1)}, u32[]{:S(2)}) copy-start(bf16[1,128,512]{2,1,0:T(8,128)(2,1)} %param.8) | copy-start | bytes 393220
  33.4 26.8 %copy-start.28 = (bf16[1,128,512]{2,1,0:T(8,128)(2,1)S(1)}, bf16[1,128,512]{2,1,0:T(8,128)(2,1)}, u32[]{:S(2)}) copy-start(bf16[1,128,512]{2,1,0:T(8,128)(2,1)} %param.9) | copy-start | bytes 393220
  33.4 20.4 %all-to-all-start.3 = ((bf16[128,32,128]{0,2,1:T(8,128)(2,1)}), bf16[128,32,128]{0,2,1:T(8,128)(2,1)}, u32[]{:S(2)}, u32[]{:S(2)}) async-start(bf16[128,32,128]{0,2,1:T(8,128)(2,1)} %bitcast.18), calls=%async_computation.3 | async-start | bytes 2097152 | tf_op jit(solution)/shard_map/all_to_all | solution.py:96
  53.9 19.3 %all-to-all-start.2 = ((bf16[128,32,128]{0,2,1:T(8,128)(2,1)}), bf16[128,32,128]{0,2,1:T(8,128)(2,1)S(1)}, u32[]{:S(2)}, u32[]{:S(2)}) async-start(bf16[128,32,128]{0,2,1:T(8,128)(2,1)} %bitcast.12), calls=%async_computation.2 | async-start | bytes 2097152 | tf_op jit(solution)/shard_map/all_to_all | solution.py:97
  73.2 1.7 copy-start.9
  74.9 43.7 %all-to-all-start = ((bf16[128,32,256]{2,0,1:T(8,128)(2,1)}), bf16[128,32,256]{2,0,1:T(8,128)(2,1)S(1)}, u32[]{:S(2)}, u32[]{:S(2)}) async-start(bf16[128,32,256]{2,0,1:T(8,128)(2,1)} %bitcast.409), calls=%async_computation | async-start | bytes 4194304 | tf_op jit(solution)/shard_map/all_to_all | solution.py:98
  81.1 412.6 %all-reduce.3.cloned.1.call-start = ((), (), s32[]{:S(2)}) async-start(), calls=%async_computation.6 | async-start | bytes 20971520
  118.5 3.0 copy-start.37
  122.8 1.6 copy-start.24
  122.8 2.0 copy-start.22
  122.8 2.0 copy-start.48
  124.9 1.1 copy-start.36
  127.6 1.5 copy-start.21
  127.6 1.5 copy-start.47
  128.5 1.4 copy-start.12
  132.8 2.5 copy-start.10
  132.8 1.0 copy-start.20
  138.7 1.5 copy-start.7
  138.7 1.5 copy-start.18
  138.7 1.5 copy-start.45
  142.1 1.2 copy-start.40
  145.3 1.7 copy-start.5
  145.3 1.7 copy-start.17
  145.4 1.7 copy-start.44
  148.2 1.0 copy-start.32
  149.3 1.3 copy-start.39
  152.8 1.8 copy-start.1
  152.8 1.8 copy-start.43
  155.9 1.2 copy-start.49
  155.9 1.2 copy-start.29
  157.1 1.5 copy-start.50
  157.1 1.5 copy-start.30
  157.1 1.5 copy-start.38
  162.0 2.0 copy-start.3
  162.0 2.2 copy-start.31
  164.0 1.1 copy-start.25
  164.0 1.3 copy-start.26
  207.2 5.0 copy-start.11
  208.7 4.0 copy-start.8
  212.2 1.9 copy-start.6
  212.7 2.6 copy-start.2
  215.4 2.2 copy-start.4
  218.5 28.0 %copy-start.23 = (bf16[128,4,128]{2,0,1:T(8,128)(2,1)S(1)}, bf16[128,4,128]{2,0,1:T(8,128)(2,1)}, u32[]{:S(2)}) copy-start(bf16[128,4,128]{2,0,1:T(8,128)(2,1)} %get-tuple-element.41) | copy-start | bytes 393220
  219.9 24.6 %all-to-all-start.4 = ((bf16[32,128,128]{1,2,0:T(8,128)(2,1)}), bf16[32,128,128]{1,2,0:T(8,128)(2,1)S(1)}, u32[]{:S(2)}, u32[]{:S(2)}) async-start(bf16[32,128,128]{1,2,0:T(8,128)(2,1)} %copy.80), calls=%async_computation.4 | async-start | bytes 2097152 | tf_op jit(solution)/shard_map/all_to_all | solution.py:104
  (9 other events, 8.3 us)
Sparse Core Ops, SparseCore 0:
  207.4 286.2 all-reduce.2
where the time goes:
time: 507 us; the launch traced here: 503 us
  waiting for transfers between devices  302 us (60%)
  local copies, waits for them, and re-layouts  55.8 us (11%)
  matrix products  49.5 us (10%)
  starting transfers between devices  34.8 us (7%)
  blocking collectives  32 us (6%)
  between operations  15.1 us (3%)
  other arithmetic  13.3 us (3%)
    unnamed x2, waiting for transfers between devices  246 us
    all_to_all x1, blocking collectives, per_device(): lax.all_to_all(partial_value.reshape(sequence_workers, token_rows, 2 * HE...  32 us
    unnamed x111, local copies, waits for them, and re-layouts  19.7 us
    all_to_all x1, waiting for transfers between devices, per_device(): lax.all_to_all(query_grads.reshape(sequence_workers, token_rows, head_wid...  18.2 us
    slice x9, local copies, waits for them, and re-layouts, attend_backward(): grad_rows = grad_heads[first_query:end_query]  15.5 us
    slice x9, local copies, waits for them, and re-layouts, attend_backward(): query_rows = query_heads[first_query:end_query]  14.9 us
    all_to_all x1, waiting for transfers between devices, per_device(): lax.all_to_all(query_send, 'seq', split_axis=1, concat_axis=0, tiled=True)  13.5 us
    all_to_all x1, waiting for transfers between devices, per_device(): lax.all_to_all(grad_send, 'seq', split_axis=1, concat_axis=0, tiled=True)  12.7 us
  transfers between devices with their start and end apart: 6, of which 5 were waited for; matrix products, arithmetic and copies ran while one was open for 11% of the time, Pallas kernels for 0%

commit v1 on v0

v1 whole, which is shorter than its diff:
```python
import functools
import jax, jax.numpy as jnp
from jax import lax
from jax.sharding import Mesh, PartitionSpec as P
from jax.experimental import pallas as pl
from jax.experimental.pallas import tpu as pltpu
bf=jnp.bfloat16; f32=jnp.float32
HEADS=8; D=128; ROWS=128; LANES=HEADS*ROWS
SCALE=D**-0.5
LOG=SCALE*1.4426950408889634
def dot(a,b,ca,cb):
    return lax.dot_general(a,b,(((ca,),(cb,)),((),())),preferred_element_type=f32)

def attn_kernel(C, pos, qg, k, v, dq, dk, dv, qt, gt, qn, gn, kt, S, E, dka, dva, dqt):
    T=k.shape[0]
    for t in range(T//128):
        kt[:,t*128:(t+1)*128]=k[t*128:(t+1)*128,:].T
    dka[...]=jnp.zeros_like(dka)
    dva[...]=jnp.zeros_like(dva)
    def block(b,carry):
        i=pos[b]
        for h in range(HEADS):
            cs=slice(h*128,(h+1)*128)
            qh=qg[b,:,cs]
            qt[:,cs]=qh.T
            qn[cs,:]=qh
        d3=qg[b,:,2048+256:2048+384].astype(f32).T
        d8=d3[0:8]+d3[8:16]+d3[16:24]
        delta=jnp.concatenate([d8[h:h+1] for h in range(HEADS)],axis=1)
        n=i//(C//128)
        def score(ch,w):
            at=pl.ds(pl.multiple_of(ch*w,w),w)
            return dot(k[at,:],qt[...],1,0)
        def p1(ch,m):
            s=score(ch,C)
            S[pl.ds(pl.multiple_of(ch*C,C),C),:]=s
            return jnp.maximum(m,jnp.max(s.reshape(C//8,8,LANES),axis=0))
        m=lax.fori_loop(0,n,p1,jnp.full((8,LANES),-1e30,f32))
        s=score(n,C)
        key=n*C+lax.broadcasted_iota(jnp.int32,(C,LANES),0)
        qp=i*128+lax.rem(lax.broadcasted_iota(jnp.int32,(C,LANES),1),128)
        s=jnp.where(key<=qp,s,-1e30)
        S[pl.ds(pl.multiple_of(n*C,C),C),:]=s
        m=jnp.maximum(m,jnp.max(s.reshape(C//8,8,LANES),axis=0))
        mc=jnp.max(m,axis=0,keepdims=True)*LOG
        def p2(ch,l):
            at=pl.ds(pl.multiple_of(ch*C,C),C)
            e=jnp.exp2(S[at,:]*LOG-mc)
            E[at,:]=e.astype(bf)
            return l+jnp.sum(e.reshape(C//8,8,LANES),axis=0)
        l=lax.fori_loop(0,n+1,p2,jnp.zeros((8,LANES),f32))
        r=1.0/jnp.sum(l,axis=0,keepdims=True)
        dr=delta*r
        for h in range(HEADS):
            cs=slice(h*128,(h+1)*128)
            gh=(qg[b,:,1024+h*128:1024+(h+1)*128].astype(f32).T*r[:,cs]).astype(bf)
            gt[:,cs]=gh
            gn[cs,:]=gh.T
        dqt[...]=jnp.zeros_like(dqt)
        def p3(ch,c):
            at=pl.ds(pl.multiple_of(ch*C,C),C)
            e=E[at,:]
            dp=dot(v[at,:],gt[...],1,0)
            ds=(e.astype(f32)*(dp-dr)).astype(bf)
            dva[at,:]+=dot(e,gn[...],1,0)
            dka[at,:]+=dot(ds,qn[...],1,0)
            dqt[...]+=dot(kt[:,at],ds,1,0)
            return c
        lax.fori_loop(0,n+1,p3,0)
        for h in range(HEADS):
            cs=slice(h*128,(h+1)*128)
            dq[b,:,cs]=(dqt[:,cs].T*SCALE).astype(bf)
        return carry
    lax.fori_loop(0,4,block,0)
    dk[...]=(dka[...]*SCALE).astype(bf)
    dv[...]=dva[...].astype(bf)

def attn(pos,qg,k,v,C=512):
    T=k.shape[0]
    vm=pl.BlockSpec(memory_space=pltpu.VMEM)
    return pl.pallas_call(functools.partial(attn_kernel, C),
        out_shape=(jax.ShapeDtypeStruct((4,128,1024),bf),jax.ShapeDtypeStruct((T,128),bf),jax.ShapeDtypeStruct((T,128),bf)),
        in_specs=[pl.BlockSpec(memory_space=pltpu.SMEM),vm,vm,vm],out_specs=(vm,vm,vm),
        scratch_shapes=[pltpu.VMEM((128,LANES),bf),pltpu.VMEM((128,LANES),bf),pltpu.VMEM((LANES,128),bf),pltpu.VMEM((LANES,128),bf),
          pltpu.VMEM((128,T),bf),pltpu.VMEM((T,LANES),f32),pltpu.VMEM((T,LANES),bf),pltpu.VMEM((T,128),f32),pltpu.VMEM((T,128),f32),pltpu.VMEM((128,LANES),f32)],
        compiler_params=pltpu.CompilerParams(vmem_limit_bytes=60<<20),name="attention_backward")(pos,qg,k,v)


def per_device(x_in, q, k, v, o, g):
    j = lax.axis_index("x")
    z = lax.axis_index("z")
    y = lax.axis_index("y")
    q, g, o, k, v, x_in = (a[0] for a in (q, g, o, k, v, x_in))
    delta = jnp.sum((g.astype(f32) * o.astype(f32)).reshape(ROWS, 4, HEADS, D), axis=3)
    d0 = delta.astype(bf)
    r1 = delta - d0.astype(f32)
    d1 = r1.astype(bf)
    d2 = (r1 - d1.astype(f32)).astype(bf)
    parts = [q.reshape(ROWS, 4, LANES), g.reshape(ROWS, 4, LANES), k.reshape(ROWS, 4, D), v.reshape(ROWS, 4, D),
             d0, d1, d2, jnp.zeros((ROWS, 4, 104), bf)]
    send = jnp.concatenate(parts, axis=2).transpose(1, 0, 2)
    x_send = x_in.reshape(ROWS, 4, -1).transpose(1, 0, 2)

    def perm(d):
        return [(x * 2 + zz, ((x + d) % 4) * 2 + (zz ^ (x & 1))) for x in range(4) for zz in range(2)]

    def back(d):
        return [(b, a) for a, b in perm(d)]

    def pick(a, i):
        return lax.dynamic_index_in_dim(a, i, 0, keepdims=False)

    got = jnp.stack([lax.ppermute(pick(send, (j + d) % 4), ("x", "z"), perm(d)) for d in range(4)])
    x_got = [lax.ppermute(pick(x_send, (j + d) % 4), ("x", "z"), perm(d)) for d in range(4)]
    pos = jnp.stack([8 * s + 4 * (z ^ (s & 1)) + y for s in [(j - d) % 4 for d in range(4)]]).astype(jnp.int32)

    def by_source(a):
        return jnp.stack([pick(a, (j - s) % 4) for s in range(4)])

    kv = by_source(got[:, :, 2 * LANES:2 * LANES + 2 * D])
    kv = lax.all_gather(kv, ("z", "y"), axis=0, tiled=False).reshape(2, 4, 4, ROWS, 2 * D)
    kv = jnp.stack([kv[::-1, :, s] if s % 2 else kv[:, :, s] for s in range(4)]).reshape(-1, 2 * D)
    dq, dk, dv = attn(pos, got, kv[:, :D], kv[:, D:])
    dqb = [lax.ppermute(dq[d], ("x", "z"), back(d)) for d in range(4)]
    dkv = jnp.concatenate([dk, dv], axis=1).reshape(4, 2, 4, ROWS, 2 * D)
    dkv = jnp.stack([dkv[s, ::-1] if s % 2 else dkv[s] for s in range(4)], axis=2).reshape(8, 4, ROWS, 2 * D)
    dkv = lax.all_to_all(dkv, ("z", "y"), 0, 0, tiled=True).astype(f32).sum(axis=0).astype(bf)
    dkvb = [lax.ppermute(pick(dkv, (j - d) % 4), ("x", "z"), back(d)) for d in range(4)]

    def by_group(parts):
        a = jnp.stack(parts)
        return jnp.stack([pick(a, (s - j) % 4) for s in range(4)], axis=1)

    dq_out = by_group(dqb).reshape(1, ROWS, -1)
    dkv_out = by_group(dkvb)
    dk_out = dkv_out[:, :, :D].reshape(1, ROWS, -1)
    dv_out = dkv_out[:, :, D:].reshape(1, ROWS, -1)
    dv_all = lax.all_gather(dkv[:, :, D:], "x", axis=0, tiled=False)
    dv_all = dv_all.transpose(1, 2, 0, 3).reshape(4 * ROWS, 4 * D)
    x_all = by_source(jnp.stack(x_got)).reshape(4 * ROWS, -1)
    w = dot(x_all, dv_all, 0, 0).astype(bf)
    w = lax.all_to_all(w.reshape(64, -1, 4 * D), ("z", "y", "h", "c"), 0, 0, tiled=True)
    return dq_out, dk_out, dv_out, w.astype(f32).sum(axis=0)


def solution(mesh):
    fine = Mesh(mesh.devices.reshape(4, 2, 4, 4, 2), ("x", "z", "y", "h", "c"))
    seq, dp = ("x", "z", "y"), ("h", "c")
    rows = P(dp, seq, None)
    return jax.shard_map(per_device, mesh=fine, in_specs=(rows,) * 6,
                         out_specs=(rows, rows, rows, P(seq + dp, None)), check_vma=False)
```

time: 507 us -> 331 us (0.65)
  waiting for transfers between devices: 302 us -> 168 us
  matrix products: 49.5 us -> 2.19 us
  Pallas kernels: 0 us -> 40.5 us
  blocking collectives: 32 us -> 12.8 us
  local copies, waits for them, and re-layouts: 55.8 us -> 38.2 us
  starting transfers between devices: 34.8 us -> 41.5 us
    unnamed x2 -> x1, waiting for transfers between devices: 246 us -> 0.02 us
    ppermute x0 -> x16, waiting for transfers between devices: none -> 122 us  [the longest x4 48.8 us: per_device(): lax.ppermute(pick(send, (j + d) % 4), ('x', 'z'), perm(d))]
    all_to_all x5 -> x2, waiting for transfers between devices: 56 us -> 0.01 us  [the longest x1 0.01 us: per_device(): lax.all_to_all(dkv, ('z', 'y'), 0, 0, tiled=True).astype(f32).sum(axis=0)]
    dot_general x41 -> x1, matrix products: 49.5 us -> 2.19 us  [dot(): lax.dot_general(a, b, (((ca,), (cb,)), ((), ())), preferred_element_type=...]
    all_gather x0 -> x1, waiting for transfers between devices: none -> 46.1 us  [per_device(): lax.all_gather(kv, ('z', 'y'), axis=0, tiled=False)]
    pallas_call x0 -> x1, Pallas kernels: none -> 40.5 us  [attn(): pl.pallas_call(functools.partial(attn_kernel, C), out_shape=(jax.ShapeDty...]
    all_to_all x1 -> x0, blocking collectives: 32 us -> none  [per_device(): lax.all_to_all(partial_value.reshape(sequence_workers, token_rows, 2 * HE...]
    slice x21 -> x7, local copies, waits for them, and re-layouts: 32.3 us -> 1.94 us  [the longest x1 1.45 us: per_device(): dq, dk, dv = attn(pos, got, kv[:, :D], kv[:, D:])]
  transfers between devices with their start and end apart: 6 -> 19, of which waited for: 5 -> 12; matrix products, arithmetic and copies ran while one was open for 11% -> 6% of each run, Pallas kernels for 0% -> 0%
where the time goes in v1:
time: 331 us; the launch traced here: 329 us
  waiting for transfers between devices  168 us (51%)
  starting transfers between devices  41.5 us (13%)
  Pallas kernels  40.5 us (12%)
  local copies, waits for them, and re-layouts  38.2 us (12%)
  between operations  14.6 us (4%)
  blocking collectives  12.8 us (4%)
  other arithmetic  10.4 us (3%)
    ppermute x4, waiting for transfers between devices, per_device(): lax.ppermute(pick(send, (j + d) % 4), ('x', 'z'), perm(d))  48.8 us
    all_gather x1, waiting for transfers between devices, per_device(): lax.all_gather(kv, ('z', 'y'), axis=0, tiled=False)  46.1 us
    ppermute x4, waiting for transfers between devices, per_device(): dqb = [lax.ppermute(dq[d], ('x', 'z'), back(d)) for d in range(4)]  41.2 us
    pallas_call x1, Pallas kernels, attn(): pl.pallas_call(functools.partial(attn_kernel, C), out_shape=(jax.ShapeDty...  40.5 us
    ppermute x4, waiting for transfers between devices, per_device(): lax.ppermute(pick(x_send, (j + d) % 4), ('x', 'z'), perm(d))  32.2 us
    all_gather x1, blocking collectives, per_device(): dv_all = lax.all_gather(dkv[:, :, D:], 'x', axis=0, tiled=False)  12.8 us
    all_to_all x1, starting transfers between devices, per_device(): lax.all_to_all(w.reshape(64, -1, 4 * D), ('z', 'y', 'h', 'c'), 0, 0, tile...  9.67 us
    unnamed x26, local copies, waits for them, and re-layouts  8.36 us
  transfers between devices with their start and end apart: 19, of which 12 were waited for; matrix products, arithmetic and copies ran while one was open for 6% of the time, Pallas kernels for 0%

profile of v1, /device:TPU:6, one launch (start us, length us, event | category | flops | bytes accessed | tf_op | source)
XLA Modules:
  0.0 328.5 jit_solution(11208935975227453696)
XLA Ops:
  7.3 1.9 reshape_squeeze.15
  10.4 1.3 copy.74
  13.1 1.5 multiply_bitcast_fusion
  18.9 3.7 %concatenate.7 = bf16[128,4,2432]{2,0,1:T(8,128)(2,1)S(1)} concatenate(bf16[128,4,1024]{2,0,1:T(8,128)(2,1)S(1)} %copy.73, bf16[128,4,1024]{2,0,1:T(8,128)(2,1)} %copy.74, bf16[128,4,128]{2,0,1:T(8,128)(2,1)} %copy.75, bf16[128,4,128]{2,0,1:T(8,128)(2,1)} %copy.76, bf16[128,4,8]{2,0,1:T(8,128)(2,1)} %copy.77, bf16[128,4,8]{2,0,1:T(8,128)(2,1)} %copy.78, ...), dimensions={2} | concatenate | bytes 4980736 | tf_op jit(solution)/shard_map/concatenate | solution.py:101
  22.7 1.3 dynamic-slice_bitcast_fusion.3
  24.0 2.2 collective-permute-start.3
  26.2 2.4 collective-permute-start.2
  29.4 2.0 collective-permute-start
  31.4 20.5 %collective-permute-done.3 = bf16[128,2432]{1,0:T(8,128)(2,1)S(1)} collective-permute-done((bf16[128,2432]{1,0:T(8,128)(2,1)}, bf16[128,2432]{1,0:T(8,128)(2,1)S(1)}, u32[]{:S(2)}, u32[]{:S(2)}) %collective-permute-start.3) | collective-permute-done | bytes 622624 | tf_op jit(solution)/shard_map/ppermute | solution.py:113
  52.0 5.1 %collective-permute-done.2 = bf16[128,2432]{1,0:T(8,128)(2,1)S(1)} collective-permute-done((bf16[128,2432]{1,0:T(8,128)(2,1)}, bf16[128,2432]{1,0:T(8,128)(2,1)S(1)}, u32[]{:S(2)}, u32[]{:S(2)}) %collective-permute-start.2) | collective-permute-done | bytes 622624 | tf_op jit(solution)/shard_map/ppermute | solution.py:113
  57.0 10.5 %collective-permute-done.1 = bf16[128,2432]{1,0:T(8,128)(2,1)S(1)} collective-permute-done((bf16[128,2432]{1,0:T(8,128)(2,1)}, bf16[128,2432]{1,0:T(8,128)(2,1)S(1)}, u32[]{:S(2)}, u32[]{:S(2)}) %collective-permute-start.1) | collective-permute-done | bytes 622624 | tf_op jit(solution)/shard_map/ppermute | solution.py:113
  67.6 12.7 %collective-permute-done = bf16[128,2432]{1,0:T(8,128)(2,1)S(1)} collective-permute-done((bf16[128,2432]{1,0:T(8,128)(2,1)S(1)}, bf16[128,2432]{1,0:T(8,128)(2,1)S(1)}, u32[]{:S(2)}, u32[]{:S(2)}) %collective-permute-start) | collective-permute-done | bytes 622624 | tf_op jit(solution)/shard_map/ppermute | solution.py:113
  81.1 1.8 pad_maximum_fusion.qg
  84.5 46.1 %all-gather.4.cloned.1.call-done = bf16[32,128,256]{2,1,0:T(8,128)(2,1)} async-done(((bf16[4,128,256]{2,1,0:T(8,128)(2,1)}), bf16[32,128,256]{2,1,0:T(8,128)(2,1)}) %all-gather.4.cloned.1.call-update) | async-done | bytes 2097168 | tf_op jit(solution)/shard_map/all_gather | solution.py:121
  130.7 1.7 slice_bitcast_fusion.3
  132.7 1.5 fusion.4
  134.2 40.5 %attention_backward.1 = (bf16[4,128,1024]{2,1,0:T(8,128)(2,1)}, bf16[4096,128]{1,0:T(8,128)(2,1)}, bf16[4096,128]{1,0:T(8,128)(2,1)}) custom-call(s32[4]{0:T(128)} %pad_add_fusion.pos, bf16[4,128,2432]{2,1,0:T(8,128)(2,1)} %copy-done, bf16[4096,128]{1,0:T(8,128)(2,1)} %get-tuple-element.31.k, bf16[4096,128]{1,0:T(8,128)(2,1)} %get-tuple-element.30.v), custom_call_target="tpu_custom_call" | custom-call | tf_op jit(solution)/shard_map/attention_backward/pallas_call | solution.py:81
  174.6 1.5 constant_dynamic-update-slice_fusion.1
  176.7 1.6 pad_maximum_fusion.2
  178.2 3.8 %all-to-all-start = ((bf16[8,4,128,256]{3,2,1,0:T(8,128)(2,1)}), bf16[8,4,128,256]{3,2,1,0:T(8,128)(2,1)S(1)}, u32[]{:S(2)}, u32[]{:S(2)}) async-start(bf16[8,4,128,256]{3,2,1,0:T(8,128)(2,1)} %pad_maximum_fusion.2), calls=%async_computation | async-start | bytes 4194304 | tf_op jit(solution)/shard_map/all_to_all | solution.py:127
  182.0 1.8 copy.89
  183.8 1.1 constant_dynamic-slice_fusion.7
  184.9 1.9 copy.93
  186.8 2.0 collective-permute-start.15
  188.8 1.9 copy.92
  191.6 1.9 copy.91
  193.5 2.4 collective-permute-start.13
  196.7 2.2 collective-permute-start.12
  198.9 14.0 %collective-permute-done.15 = bf16[128,1280]{1,0:T(8,128)(2,1)S(1)} collective-permute-done((bf16[128,1280]{1,0:T(8,128)(2,1)}, bf16[128,1280]{1,0:T(8,128)(2,1)S(1)}, u32[]{:S(2)}, u32[]{:S(2)}) %collective-permute-start.15) | collective-permute-done | bytes 327712 | tf_op jit(solution)/shard_map/ppermute | solution.py:114
  212.9 10.1 %collective-permute-done.14 = bf16[128,1280]{1,0:T(8,128)(2,1)S(1)} collective-permute-done((bf16[128,1280]{1,0:T(8,128)(2,1)}, bf16[128,1280]{1,0:T(8,128)(2,1)S(1)}, u32[]{:S(2)}, u32[]{:S(2)}) %collective-permute-start.14) | collective-permute-done | bytes 327712 | tf_op jit(solution)/shard_map/ppermute | solution.py:114
  223.0 2.5 collective-permute-done.13
  225.5 5.6 %collective-permute-done.12 = bf16[128,1280]{1,0:T(8,128)(2,1)S(1)} collective-permute-done((bf16[128,1280]{1,0:T(8,128)(2,1)}, bf16[128,1280]{1,0:T(8,128)(2,1)S(1)}, u32[]{:S(2)}, u32[]{:S(2)}) %collective-permute-start.12) | collective-permute-done | bytes 327712 | tf_op jit(solution)/shard_map/ppermute | solution.py:114
  231.4 1.3 pad_maximum_fusion.4
  233.0 12.8 %all-gather.1 = bf16[16,128,128]{2,1,0:T(8,128)(2,1)S(1)} all-gather(bf16[4,128,128]{2,1,0:T(8,128)(2,1)S(1)} %slice.95), channel_id=3, replica_groups=mesh['x'=4,'z'=2,'y'=4,'h'=4,'c'=2] {'x'}, dimensions={0}, use_global_device_ids=true | all-gather | bytes 655360 | tf_op jit(solution)/shard_map/all_gather | solution.py:138
  246.2 2.2 convolution_convert_fusion
  248.4 1.3 reshape.85
  249.7 9.7 %all-to-all-start.1 = ((bf16[64,20,512]{2,1,0:T(8,128)(2,1)}), bf16[64,20,512]{2,1,0:T(8,128)(2,1)S(1)}, u32[]{:S(2)}, u32[]{:S(2)}) async-start(bf16[64,20,512]{2,1,0:T(8,128)(2,1)} %reshape.85), calls=%async_computation.1 | async-start | bytes 3145728 | tf_op jit(solution)/shard_map/all_to_all | solution.py:142
  260.3 2.6 collective-permute-start.6
  262.9 1.4 collective-permute-start.5
  264.3 2.3 collective-permute-start.4
  266.6 33.4 %collective-permute-done.7 = bf16[128,1024]{1,0:T(8,128)(2,1)S(1)} collective-permute-done((bf16[128,1024]{1,0:T(8,128)(2,1)}, bf16[128,1024]{1,0:T(8,128)(2,1)S(1)}, u32[]{:S(2)}, u32[]{:S(2)}) %collective-permute-start.7) | collective-permute-done | bytes 262176 | tf_op jit(solution)/shard_map/ppermute | solution.py:124
  300.0 3.6 %collective-permute-done.6 = bf16[128,1024]{1,0:T(8,128)(2,1)S(1)} collective-permute-done((bf16[128,1024]{1,0:T(8,128)(2,1)}, bf16[128,1024]{1,0:T(8,128)(2,1)S(1)}, u32[]{:S(2)}, u32[]{:S(2)}) %collective-permute-start.6) | collective-permute-done | bytes 262176 | tf_op jit(solution)/shard_map/ppermute | solution.py:124
  303.7 4.2 %collective-permute-done.5 = bf16[128,1024]{1,0:T(8,128)(2,1)S(1)} collective-permute-done((bf16[128,1024]{1,0:T(8,128)(2,1)}, bf16[128,1024]{1,0:T(8,128)(2,1)S(1)}, u32[]{:S(2)}, u32[]{:S(2)}) %collective-permute-start.5) | collective-permute-done | bytes 262176 | tf_op jit(solution)/shard_map/ppermute | solution.py:124
  308.2 1.8 collective-permute-start.10
  310.0 1.3 collective-permute-start.9
  311.3 3.7 %collective-permute-start.8 = (bf16[128,256]{1,0:T(8,128)(2,1)S(1)}, bf16[128,256]{1,0:T(8,128)(2,1)S(1)}, u32[]{:S(2)}, u32[]{:S(2)}) collective-permute-start(bf16[128,256]{1,0:T(8,128)(2,1)S(1)} %get-tuple-element.58), channel_id=1, source_target_pairs={{0,0},{32,32},{96,64},{64,96},{128,128},{160,160},{224,192},{192,2... | collective-permute-start | bytes 196616 | tf_op jit(solution)/shard_map/ppermute | solution.py:128
  315.1 1.3 copy.84
  316.5 2.3 copy.95
  (77 shorter events, 18.0 us)
Async XLA Ops:
  7.2 123.5 %all-gather.4.cloned.1.call-start = ((), (), s32[]{:S(2)}) async-start(), calls=%async_computation.2 | async-start | bytes 2359296 | tf_op jit(solution)/shard_map/all_gather | solution.py:121
  7.3 2.3 copy-start.1
  9.5 2.1 copy-start.8
  9.6 2.8 copy-start.9
  24.0 28.0 %collective-permute-start.3 = (bf16[128,2432]{1,0:T(8,128)(2,1)}, bf16[128,2432]{1,0:T(8,128)(2,1)S(1)}, u32[]{:S(2)}, u32[]{:S(2)}) collective-permute-start(bf16[128,2432]{1,0:T(8,128)(2,1)} %get-tuple-element.23), channel_id=1, source_target_pairs={{0,192},{32,224},{64,32},{96,0},{128,64},{160,96},{192,160},{224,1... | collective-permute-start | bytes 1867784 | tf_op jit(solution)/shard_map/ppermute | solution.py:113
  26.2 30.9 %collective-permute-start.2 = (bf16[128,2432]{1,0:T(8,128)(2,1)}, bf16[128,2432]{1,0:T(8,128)(2,1)S(1)}, u32[]{:S(2)}, u32[]{:S(2)}) collective-permute-start(bf16[128,2432]{1,0:T(8,128)(2,1)} %get-tuple-element.24), channel_id=1, source_target_pairs={{0,128},{32,160},{64,224},{96,192},{128,0},{160,32},{192,96},{224,... | collective-permute-start | bytes 1867784 | tf_op jit(solution)/shard_map/ppermute | solution.py:113
  28.5 39.0 %collective-permute-start.1 = (bf16[128,2432]{1,0:T(8,128)(2,1)}, bf16[128,2432]{1,0:T(8,128)(2,1)S(1)}, u32[]{:S(2)}, u32[]{:S(2)}) collective-permute-start(bf16[128,2432]{1,0:T(8,128)(2,1)} %get-tuple-element.25), channel_id=1, source_target_pairs={{0,64},{32,96},{64,160},{96,128},{128,192},{160,224},{192,32},{224... | collective-permute-start | bytes 1867784 | tf_op jit(solution)/shard_map/ppermute | solution.py:113
  29.4 50.9 %collective-permute-start = (bf16[128,2432]{1,0:T(8,128)(2,1)S(1)}, bf16[128,2432]{1,0:T(8,128)(2,1)S(1)}, u32[]{:S(2)}, u32[]{:S(2)}) collective-permute-start(bf16[128,2432]{1,0:T(8,128)(2,1)S(1)} %get-tuple-element.22), channel_id=1, source_target_pairs={{0,0},{32,32},{64,96},{96,64},{128,128},{160,160},{192,224},{224,1... | collective-permute-start | bytes 1867784 | tf_op jit(solution)/shard_map/ppermute | solution.py:113
  57.0 23.2 %copy-start.5 = (bf16[128,2432]{1,0:T(8,128)(2,1)}, bf16[128,2432]{1,0:T(8,128)(2,1)S(1)}, u32[]{:S(2)}) copy-start(bf16[128,2432]{1,0:T(8,128)(2,1)S(1)} %collective-permute-done.2) | copy-start | bytes 1867780
  67.6 12.7 %copy-start.6 = (bf16[128,2432]{1,0:T(8,128)(2,1)}, bf16[128,2432]{1,0:T(8,128)(2,1)S(1)}, u32[]{:S(2)}) copy-start(bf16[128,2432]{1,0:T(8,128)(2,1)S(1)} %collective-permute-done.1) | copy-start | bytes 1867780
  80.2 0.9 copy-start.7
  82.9 49.4 %copy-start = (bf16[4,128,2432]{2,1,0:T(8,128)(2,1)}, bf16[4,128,2432]{2,1,0:T(8,128)(2,1)S(1)}, u32[]{:S(2)}) copy-start(bf16[4,128,2432]{2,1,0:T(8,128)(2,1)S(1)} %pad_maximum_fusion.qg) | copy-start | bytes 7471108
  174.6 1.5 copy-start.4
  178.2 54.4 %all-to-all-start = ((bf16[8,4,128,256]{3,2,1,0:T(8,128)(2,1)}), bf16[8,4,128,256]{3,2,1,0:T(8,128)(2,1)S(1)}, u32[]{:S(2)}, u32[]{:S(2)}) async-start(bf16[8,4,128,256]{3,2,1,0:T(8,128)(2,1)} %pad_maximum_fusion.2), calls=%async_computation | async-start | bytes 4194304 | tf_op jit(solution)/shard_map/all_to_all | solution.py:127
  184.9 10.9 %copy-start.2 = (bf16[128,1,1280]{0,2,1:T(8,128)(2,1)S(1)}, bf16[128,1,1280]{0,2,1:T(8,128)(2,1)}, u32[]{:S(2)}) copy-start(bf16[128,1,1280]{0,2,1:T(8,128)(2,1)} %get-tuple-element.40) | copy-start | bytes 983044
  186.8 26.1 %collective-permute-start.15 = (bf16[128,1280]{1,0:T(8,128)(2,1)}, bf16[128,1280]{1,0:T(8,128)(2,1)S(1)}, u32[]{:S(2)}, u32[]{:S(2)}) collective-permute-start(bf16[128,1280]{1,0:T(8,128)(2,1)} %bitcast.60), channel_id=1, source_target_pairs={{0,192},{32,224},{64,32},{96,0},{128,64},{160,96},{192,160},{224,1... | collective-permute-start | bytes 983048 | tf_op jit(solution)/shard_map/ppermute | solution.py:114
  190.7 32.3 %collective-permute-start.14 = (bf16[128,1280]{1,0:T(8,128)(2,1)}, bf16[128,1280]{1,0:T(8,128)(2,1)S(1)}, u32[]{:S(2)}, u32[]{:S(2)}) collective-permute-start(bf16[128,1280]{1,0:T(8,128)(2,1)} %bitcast.58), channel_id=1, source_target_pairs={{0,128},{32,160},{64,224},{96,192},{128,0},{160,32},{192,96},{224,... | collective-permute-start | bytes 983048 | tf_op jit(solution)/shard_map/ppermute | solution.py:114
  193.5 32.1 %collective-permute-start.13 = (bf16[128,1280]{1,0:T(8,128)(2,1)}, bf16[128,1280]{1,0:T(8,128)(2,1)S(1)}, u32[]{:S(2)}, u32[]{:S(2)}) collective-permute-start(bf16[128,1280]{1,0:T(8,128)(2,1)} %bitcast.135), channel_id=1, source_target_pairs={{0,64},{32,96},{64,160},{96,128},{128,192},{160,224},{192,32},{224... | collective-permute-start | bytes 983048 | tf_op jit(solution)/shard_map/ppermute | solution.py:114
  196.7 34.4 %collective-permute-start.12 = (bf16[128,1280]{1,0:T(8,128)(2,1)}, bf16[128,1280]{1,0:T(8,128)(2,1)S(1)}, u32[]{:S(2)}, u32[]{:S(2)}) collective-permute-start(bf16[128,1280]{1,0:T(8,128)(2,1)} %bitcast.136), channel_id=1, source_target_pairs={{0,0},{32,32},{64,96},{96,64},{128,128},{160,160},{192,224},{224,1... | collective-permute-start | bytes 983048 | tf_op jit(solution)/shard_map/ppermute | solution.py:114
  249.7 9.7 %copy-start.3 = (bf16[4,128,1024]{2,1,0:T(8,128)(2,1)S(1)}, bf16[4,128,1024]{2,1,0:T(8,128)(2,1)}, u32[]{:S(2)}) copy-start(bf16[4,128,1024]{2,1,0:T(8,128)(2,1)} %get-tuple-element.7) | copy-start | bytes 3145732
  249.7 71.0 %all-to-all-start.1 = ((bf16[64,20,512]{2,1,0:T(8,128)(2,1)}), bf16[64,20,512]{2,1,0:T(8,128)(2,1)S(1)}, u32[]{:S(2)}, u32[]{:S(2)}) async-start(bf16[64,20,512]{2,1,0:T(8,128)(2,1)} %reshape.85), calls=%async_computation.1 | async-start | bytes 3145728 | tf_op jit(solution)/shard_map/all_to_all | solution.py:142
  260.3 39.7 %collective-permute-start.7 = (bf16[128,1024]{1,0:T(8,128)(2,1)}, bf16[128,1024]{1,0:T(8,128)(2,1)S(1)}, u32[]{:S(2)}, u32[]{:S(2)}) collective-permute-start(bf16[128,1024]{1,0:T(8,128)(2,1)} %get-tuple-element.49), channel_id=1, source_target_pairs={{192,0},{224,32},{32,64},{0,96},{64,128},{96,160},{160,192},{128,2... | collective-permute-start | bytes 786440 | tf_op jit(solution)/shard_map/ppermute | solution.py:124
  260.3 43.3 %collective-permute-start.6 = (bf16[128,1024]{1,0:T(8,128)(2,1)}, bf16[128,1024]{1,0:T(8,128)(2,1)S(1)}, u32[]{:S(2)}, u32[]{:S(2)}) collective-permute-start(bf16[128,1024]{1,0:T(8,128)(2,1)} %get-tuple-element.50), channel_id=1, source_target_pairs={{128,0},{160,32},{224,64},{192,96},{0,128},{32,160},{96,192},{64,2... | collective-permute-start | bytes 786440 | tf_op jit(solution)/shard_map/ppermute | solution.py:124
  262.9 44.9 %collective-permute-start.5 = (bf16[128,1024]{1,0:T(8,128)(2,1)}, bf16[128,1024]{1,0:T(8,128)(2,1)S(1)}, u32[]{:S(2)}, u32[]{:S(2)}) collective-permute-start(bf16[128,1024]{1,0:T(8,128)(2,1)} %get-tuple-element.51), channel_id=1, source_target_pairs={{64,0},{96,32},{160,64},{128,96},{192,128},{224,160},{32,192},{0,2... | collective-permute-start | bytes 786440 | tf_op jit(solution)/shard_map/ppermute | solution.py:124
  264.3 43.5 %collective-permute-start.4 = (bf16[128,1024]{1,0:T(8,128)(2,1)S(1)}, bf16[128,1024]{1,0:T(8,128)(2,1)S(1)}, u32[]{:S(2)}, u32[]{:S(2)}) collective-permute-start(bf16[128,1024]{1,0:T(8,128)(2,1)S(1)} %get-tuple-element.48), channel_id=1, source_target_pairs={{0,0},{32,32},{96,64},{64,96},{128,128},{160,160},{224,192},{192,2... | collective-permute-start | bytes 786440 | tf_op jit(solution)/shard_map/ppermute | solution.py:124
  308.1 10.7 %collective-permute-start.11 = (bf16[128,256]{1,0:T(8,128)(2,1)S(1)}, bf16[128,256]{1,0:T(8,128)(2,1)S(1)}, u32[]{:S(2)}, u32[]{:S(2)}) collective-permute-start(bf16[128,256]{1,0:T(8,128)(2,1)S(1)} %get-tuple-element.59), channel_id=1, source_target_pairs={{192,0},{224,32},{32,64},{0,96},{64,128},{96,160},{160,192},{128,2... | collective-permute-start | bytes 196616 | tf_op jit(solution)/shard_map/ppermute | solution.py:128
  308.2 10.6 %collective-permute-start.10 = (bf16[128,256]{1,0:T(8,128)(2,1)S(1)}, bf16[128,256]{1,0:T(8,128)(2,1)S(1)}, u32[]{:S(2)}, u32[]{:S(2)}) collective-permute-start(bf16[128,256]{1,0:T(8,128)(2,1)S(1)} %get-tuple-element.60), channel_id=1, source_target_pairs={{128,0},{160,32},{224,64},{192,96},{0,128},{32,160},{96,192},{64,2... | collective-permute-start | bytes 196616 | tf_op jit(solution)/shard_map/ppermute | solution.py:128
  310.0 8.8 %collective-permute-start.9 = (bf16[128,256]{1,0:T(8,128)(2,1)S(1)}, bf16[128,256]{1,0:T(8,128)(2,1)S(1)}, u32[]{:S(2)}, u32[]{:S(2)}) collective-permute-start(bf16[128,256]{1,0:T(8,128)(2,1)S(1)} %get-tuple-element.61), channel_id=1, source_target_pairs={{64,0},{96,32},{160,64},{128,96},{192,128},{224,160},{32,192},{0,2... | collective-permute-start | bytes 196616 | tf_op jit(solution)/shard_map/ppermute | solution.py:128
  311.3 7.5 %collective-permute-start.8 = (bf16[128,256]{1,0:T(8,128)(2,1)S(1)}, bf16[128,256]{1,0:T(8,128)(2,1)S(1)}, u32[]{:S(2)}, u32[]{:S(2)}) collective-permute-start(bf16[128,256]{1,0:T(8,128)(2,1)S(1)} %get-tuple-element.58), channel_id=1, source_target_pairs={{0,0},{32,32},{96,64},{64,96},{128,128},{160,160},{224,192},{192,2... | collective-permute-start | bytes 196616 | tf_op jit(solution)/shard_map/ppermute | solution.py:128
Sparse Core Ops, SparseCore 0:
  84.0 46.6 all-gather.3

commit v2 on v1

v2 whole, which is shorter than its diff:
```python
import jax
import jax.numpy as jnp
from jax import lax
from jax.sharding import Mesh, PartitionSpec as P
from jax.experimental import pallas as pl
from jax.experimental.pallas import tpu as pltpu

bf = jnp.bfloat16
f32 = jnp.float32
HEADS = 8
D = 128
ROWS = 128
LANES = HEADS * ROWS
SCALE = D ** -0.5
LOG = SCALE * 1.4426950408889634
CHUNK = 512
BLOCKS = CHUNK // ROWS
XCOLS = 1280


def dot(a, b, ca, cb):
    return lax.dot_general(a, b, (((ca,), (cb,)), ((), ())), preferred_element_type=f32)


def cols(index, width):
    return pl.ds(pl.multiple_of(index * width, width), width)


def remote(src, dst, sems, at, peer):
    return pltpu.make_async_remote_copy(src_ref=src, dst_ref=dst, send_sem=sems[0].at[at], recv_sem=sems[1].at[at],
                                        device_id=peer, device_id_type=pl.DeviceIdType.MESH)


def arrived(ref, sem):
    pltpu.make_async_copy(ref, ref, sem).wait()


def kernel(q, g, o, k, v, xin, dqo, dko, dvo, xr, dvall,
           kv, kt, qr, gr, dr, gl, ol, dl, qt, gt, qn, gn, S, E, dka, dva, dqt, dqv, part, rcv, fin,
           *sems):
    (lg, lo), sk, sv, sq, sg, sd, sx, sb, sc, sdq, sp, srk, srv, sdv = [sems[i:i + 2] for i in range(0, 28, 2)]
    x, z, y = (lax.axis_index(a) for a in ("x", "z", "y"))
    me = 8 * x + 4 * z + y
    xs = [lax.rem(x + d, 4) for d in range(4)]
    ys = [lax.rem(y + e, 4) for e in range(4)]
    plane = [(dz, e) for dz in range(2) for e in range(4) if dz or e]

    def in_plane(dz, e):
        return {"z": (1 - z) if dz else z, "y": ys[e]}

    barrier = pltpu.get_barrier_semaphore()
    for d in (1, 2, 3):
        pl.semaphore_signal(barrier, inc=1, device_id={"x": xs[d]}, device_id_type=pl.DeviceIdType.MESH)
    for dz, e in plane:
        pl.semaphore_signal(barrier, inc=1, device_id=in_plane(dz, e), device_id_type=pl.DeviceIdType.MESH)
    get_g = pltpu.make_async_copy(g.at[0], gl, lg)
    get_o = pltpu.make_async_copy(o.at[0], ol, lo)
    get_g.start()
    get_o.start()
    pl.semaphore_wait(barrier, 10)

    sends = []

    def send(*a):
        copy = remote(*a)
        copy.start()
        sends.append(copy)

    for src, dst, s, width in ((k.at[0], kv.at[me, :, 0:D], sk, D), (v.at[0], kv.at[me, :, D:2 * D], sv, D),
                               (q.at[0], qr.at[x], sq, LANES), (g.at[0], gr.at[x], sg, LANES)):
        for d in (1, 3, 2):
            send(src.at[:, cols(xs[d], width)], dst, s, d, {"x": xs[d]})
        pltpu.make_async_copy(src.at[:, cols(x, width)], dst, s[1].at[0]).start()

    get_g.wait()
    get_o.wait()
    head = lax.broadcasted_iota(jnp.int32, (HEADS, LANES), 0)
    ones = jnp.where(head == lax.broadcasted_iota(jnp.int32, (HEADS, LANES), 1) // D, 1.0, 0.0).astype(bf)
    for j in range(4):
        at = slice(j * LANES, (j + 1) * LANES)
        prod = gl[:, at].astype(f32) * ol[:, at].astype(f32)
        high = prod.astype(bf)
        low = (prod - high.astype(f32)).astype(bf)
        dl[j] = dot(ones, high, 1, 1) + dot(ones, low, 1, 1)
    for d in (1, 3, 2):
        send(dl.at[xs[d]], dr.at[x], sd, d, {"x": xs[d]})
    pltpu.make_async_copy(dl.at[x], dr.at[x], sd[1].at[0]).start()

    def slot(s, zz, yy):
        return kv.at[8 * s + 4 * zz + yy]

    for s in range(4):
        d = lax.rem(x + 4 - s, 4)
        mine = slot(s, z, y)
        arrived(mine.at[:, 0:D], sk[1].at[d])
        arrived(mine.at[:, D:2 * D], sv[1].at[d])
        send(mine, mine, sb, s, {"z": 1 - z})
        for e in (1, 3, 2):
            send(mine, mine, sc, (s, 0, e), {"y": ys[e]})
    for s in range(4):
        theirs = slot(s, 1 - z, y)
        arrived(theirs, sb[1].at[s])
        for e in (1, 3, 2):
            send(theirs, theirs, sc, (s, 1, e), {"y": ys[e]})
    for d in (1, 3, 2):
        send(xin.at[0, :, cols(xs[d], XCOLS)], xr.at[x], sx, d, {"x": xs[d]})
    pltpu.make_async_copy(xin.at[0, :, cols(x, XCOLS)], xr.at[x], sx[1].at[0]).start()

    dka[...] = jnp.zeros_like(dka)
    dva[...] = jnp.zeros_like(dva)

    def block(s, carry):
        d = lax.rem(x + 4 - s, 4)
        i = 8 * s + 4 * z + y
        for e in (1, 2, 3):
            yy = lax.rem(y + 4 - e, 4)
            arrived(slot(s, z, yy), sc[1].at[s, 0, e])
            arrived(slot(s, 1 - z, yy), sc[1].at[s, 1, e])
        for b in range(8):
            kt[:, cols(8 * s + b, D)] = kv[8 * s + b, :, 0:D].T
        arrived(qr.at[s], sq[1].at[d])
        arrived(gr.at[s], sg[1].at[d])
        arrived(dr.at[s], sd[1].at[d])
        for h in range(HEADS):
            cs = slice(h * D, (h + 1) * D)
            qh = qr[s, :, cs]
            qt[:, cs] = qh.T
            qn[cs, :] = qh
        delta = jnp.concatenate([dr[s, h:h + 1, :] for h in range(HEADS)], axis=1)
        n = i // BLOCKS

        def score(ch):
            keys = kv[pl.ds(ch * BLOCKS, BLOCKS), :, 0:D].reshape(CHUNK, D)
            return dot(keys, qt[...], 1, 0)

        def top(m, s):
            return jnp.maximum(m, jnp.max(s.reshape(CHUNK // 8, 8, LANES), axis=0))

        def p1(ch, m):
            s = score(ch)
            S[cols(ch, CHUNK), :] = s
            return top(m, s)

        m = lax.fori_loop(0, n, p1, jnp.full((8, LANES), -1e30, f32))
        last = score(n)
        key = n * CHUNK + lax.broadcasted_iota(jnp.int32, (CHUNK, LANES), 0)
        row = i * ROWS + lax.broadcasted_iota(jnp.int32, (CHUNK, LANES), 1) % ROWS
        last = jnp.where(key <= row, last, -1e30)
        S[cols(n, CHUNK), :] = last
        mc = jnp.max(top(m, last), axis=0, keepdims=True) * LOG

        def p2(ch, total):
            e = jnp.exp2(S[cols(ch, CHUNK), :] * LOG - mc)
            E[cols(ch, CHUNK), :] = e.astype(bf)
            return total + jnp.sum(e.reshape(CHUNK // 8, 8, LANES), axis=0)

        total = lax.fori_loop(0, n + 1, p2, jnp.zeros((8, LANES), f32))
        r = 1.0 / jnp.sum(total, axis=0, keepdims=True)
        shift = delta * r
        for h in range(HEADS):
            cs = slice(h * D, (h + 1) * D)
            gh = (gr[s, :, cs].astype(f32).T * r[:, cs]).astype(bf)
            gt[:, cs] = gh
            gn[cs, :] = gh.T
        dqt[...] = jnp.zeros_like(dqt)

        def p3(ch, c):
            at = cols(ch, CHUNK)
            e = E[at, :]
            values = kv[pl.ds(ch * BLOCKS, BLOCKS), :, D:2 * D].reshape(CHUNK, D)
            ds = (e.astype(f32) * (dot(values, gt[...], 1, 0) - shift)).astype(bf)
            dva[at, :] += dot(e, gn[...], 1, 0)
            dka[at, :] += dot(ds, qn[...], 1, 0)
            dqt[...] += dot(kt[:, at], ds, 1, 0)
            return c

        lax.fori_loop(0, n + 1, p3, 0)
        for h in range(HEADS):
            cs = slice(h * D, (h + 1) * D)
            dqv[s, :, cs] = (dqt[:, cs].T * SCALE).astype(bf)

        home = dqo.at[0, :, cols(x, LANES)]

        @pl.when(s == x)
        def _():
            pltpu.make_async_copy(dqv.at[s], home, sdq[1].at[0]).start()

        @pl.when(s != x)
        def _():
            remote(dqv.at[s], home, sdq, lax.rem(s + 4 - x, 4), {"x": s}).start()

        return carry

    lax.fori_loop(0, 4, block, 0)

    for b in range(32):
        at = slice(b * ROWS, (b + 1) * ROWS)
        part[b // 8, b % 8, :, 0:D] = (dka[at, :] * SCALE).astype(bf)
        part[b // 8, b % 8, :, D:2 * D] = dva[at, :].astype(bf)
    for dz, e in plane:
        peer = in_plane(dz, e)
        send(part.at[:, 4 * peer["z"] + peer["y"]], rcv.at[dz * 4 + e], sp, dz * 4 + e, peer)
    for s in range(4):
        fin[s] = part[s, 4 * z + y].astype(f32)
    for dz, e in plane:
        arrived(rcv.at[dz * 4 + e], sp[1].at[dz * 4 + e])
        for s in range(4):
            fin[s] += rcv[dz * 4 + e, s].astype(f32)
    for s in range(4):
        part[s, 4 * z + y] = fin[s].astype(bf)
    out = part.at[:, 4 * z + y]
    for d in (1, 3, 2):
        t = xs[d]
        send(out.at[:, :, D:2 * D], dvall.at[:, :, cols(x, D)], sdv, d, {"x": t})
        send(out.at[t, :, 0:D], dko.at[0, :, cols(x, D)], srk, d, {"x": t})
        send(out.at[t, :, D:2 * D], dvo.at[0, :, cols(x, D)], srv, d, {"x": t})
    own = [pltpu.make_async_copy(out.at[:, :, D:2 * D], dvall.at[:, :, cols(x, D)], sdv[1].at[0]),
           pltpu.make_async_copy(out.at[x, :, 0:D], dko.at[0, :, cols(x, D)], srk[1].at[0]),
           pltpu.make_async_copy(out.at[x, :, D:2 * D], dvo.at[0, :, cols(x, D)], srv[1].at[0])]
    for copy in own:
        copy.start()
    for d in range(4):
        f = lax.rem(x + 4 - d, 4)
        arrived(xr.at[f], sx[1].at[d])
        arrived(dqo.at[0, :, cols(f, LANES)], sdq[1].at[d])
        arrived(dvall.at[:, :, cols(f, D)], sdv[1].at[d])
        arrived(dko.at[0, :, cols(f, D)], srk[1].at[d])
        arrived(dvo.at[0, :, cols(f, D)], srv[1].at[d])
    for copy in sends:
        copy.wait_send()
    for d in (1, 2, 3):
        remote(dqv.at[xs[d]], dqo.at[0, :, cols(x, LANES)], sdq, d, {"x": xs[d]}).wait_send()


def whole(q, g, o, k, v, xin):
    T = 32 * ROWS
    anyspace = pl.BlockSpec(memory_space=pl.ANY)
    dma = pltpu.SemaphoreType.DMA
    shapes = [(), ()] + [(4,)] * 14 + [(4, 2, 4)] * 2 + [(4,)] * 2 + [(8,)] * 2 + [(4,)] * 6
    scratch = [((32, ROWS, 2 * D), bf), ((D, T), bf), ((4, ROWS, LANES), bf), ((4, ROWS, LANES), bf), ((4, HEADS, ROWS), f32),
               ((ROWS, 4 * LANES), bf), ((ROWS, 4 * LANES), bf), ((4, HEADS, ROWS), f32),
               ((D, LANES), bf), ((D, LANES), bf), ((LANES, D), bf), ((LANES, D), bf), ((T, LANES), f32), ((T, LANES), bf),
               ((T, D), f32), ((T, D), f32), ((D, LANES), f32), ((4, ROWS, LANES), bf), ((4, 8, ROWS, 2 * D), bf),
               ((8, 4, ROWS, 2 * D), bf), ((4, ROWS, 2 * D), f32)]
    return pl.pallas_call(
        kernel,
        out_shape=[jax.ShapeDtypeStruct(s, bf) for s in (
            (1, ROWS, 4 * LANES), (1, ROWS, 4 * D), (1, ROWS, 4 * D), (4, ROWS, XCOLS), (4, ROWS, 4 * D))],
        in_specs=[anyspace] * 6, out_specs=[anyspace] * 5,
        scratch_shapes=[pltpu.VMEM(*s) for s in scratch] + [dma(s) for s in shapes],
        compiler_params=pltpu.CompilerParams(vmem_limit_bytes=60 << 20, collective_id=0, has_side_effects=True),
        name="attention_backward")(q, g, o, k, v, xin)


def per_device(x_in, q, k, v, o, g):
    dq, dk, dv, xr, dvall = whole(q, g, o, k, v, x_in)
    w = dot(xr.reshape(4 * ROWS, XCOLS), dvall.reshape(4 * ROWS, 4 * D), 0, 0).astype(bf)
    w = lax.all_to_all(w.reshape(64, -1, 4 * D), ("z", "y", "h", "c"), 0, 0, tiled=True)
    return dq, dk, dv, w.astype(f32).sum(axis=0)


def solution(mesh):
    fine = Mesh(mesh.devices.reshape(4, 2, 4, 4, 2), ("x", "z", "y", "h", "c"))
    seq, dp = ("x", "z", "y"), ("h", "c")
    rows = P(dp, seq, None)
    return jax.shard_map(per_device, mesh=fine, in_specs=(rows,) * 6,
                         out_specs=(rows, rows, rows, P(seq + dp, None)), check_vma=False)
```

time: 331 us -> 167 us (0.50)
  waiting for transfers between devices: 168 us -> 40.8 us
  Pallas kernels: 40.5 us -> 105 us
  local copies, waits for them, and re-layouts: 38.2 us -> 3.61 us
  starting transfers between devices: 41.5 us -> 12.1 us
  between operations: 14.6 us -> 0.67 us
  blocking collectives: 12.8 us -> 0 us
  other arithmetic: 10.4 us -> 0.89 us
    ppermute x16 -> x0, waiting for transfers between devices: 122 us -> none  [the longest x4 48.8 us: per_device(): lax.ppermute(pick(send, (j + d) % 4), ('x', 'z'), perm(d))]
    pallas_call x1, Pallas kernels: 40.5 us -> 105 us  [whole(): pl.pallas_call(kernel, out_shape=[jax.ShapeDtypeStruct(s, bf) for s in ((...]
    all_gather x1 -> x0, waiting for transfers between devices: 46.1 us -> none  [per_device(): lax.all_gather(kv, ('z', 'y'), axis=0, tiled=False)]
    all_to_all x1, waiting for transfers between devices: 0.01 us -> 40.8 us  [per_device(): lax.all_to_all(w.reshape(64, -1, 4 * D), ('z', 'y', 'h', 'c'), 0, 0, tile...]
    ppermute x16 -> x0, starting transfers between devices: 28 us -> none  [the longest x4 7.44 us: per_device(): lax.ppermute(pick(x_send, (j + d) % 4), ('x', 'z'), perm(d))]
    another operation x18 -> x0, local copies, waits for them, and re-layouts: 16.6 us -> none
    all_gather x1 -> x0, blocking collectives: 12.8 us -> none  [per_device(): dv_all = lax.all_gather(dkv[:, :, D:], 'x', axis=0, tiled=False)]
    another operation x11 -> x0, other arithmetic: 6.88 us -> none  [the longest x2 2.13 us: by_source(): return jnp.stack([pick(a, (j - s) % 4) for s in range(4)])]
  transfers between devices with their start and end apart: 19 -> 1, of which waited for: 12 -> 1; matrix products, arithmetic and copies ran while one was open for 6% -> 0% of each run, Pallas kernels for 0% -> 0%
where the time goes in v2:
time: 167 us; the launch traced here: 165 us
  Pallas kernels  105 us (63%)
  waiting for transfers between devices  40.8 us (24%)
  starting transfers between devices  12.1 us (7%)
  local copies, waits for them, and re-layouts  3.61 us (2%)
  matrix products  2.31 us (1%)
    pallas_call x1, Pallas kernels, whole(): pl.pallas_call(kernel, out_shape=[jax.ShapeDtypeStruct(s, bf) for s in ((...  105 us
    all_to_all x1, waiting for transfers between devices, per_device(): lax.all_to_all(w.reshape(64, -1, 4 * D), ('z', 'y', 'h', 'c'), 0, 0, tile...  40.8 us
    all_to_all x1, starting transfers between devices, per_device(): lax.all_to_all(w.reshape(64, -1, 4 * D), ('z', 'y', 'h', 'c'), 0, 0, tile...  12.1 us
  transfers between devices with their start and end apart: 1, of which 1 were waited for; matrix products, arithmetic and copies ran while one was open for 0% of the time, Pallas kernels for 0%

profile of v2, /device:TPU:6, one launch (start us, length us, event | category | flops | bytes accessed | tf_op | source)
XLA Modules:
  0.0 165.3 jit_solution(11787322871681783361)
XLA Ops:
  0.6 104.9 %attention_backward.1 = (bf16[1,128,4096]{2,1,0:T(8,128)(2,1)}, bf16[1,128,512]{2,1,0:T(8,128)(2,1)}, bf16[1,128,512]{2,1,0:T(8,128)(2,1)}, bf16[4,128,1280]{2,1,0:T(8,128)(2,1)}, bf16[4,128,512]{2,1,0:T(8,128)(2,1)}) custom-call(bf16[1,128,4096]{2,1,0:T(8,128)(2,1)} %q.1, bf16[1,128,4096]{2,1,0:T(8,128)(2,1)} %g.1, bf16[1,128,4096]{2,1,0:T(8,128)(2,1)} %o.1, ...), custom_call_target="tpu_custom_call" | custom-call | tf_op jit(solution)/shard_map/attention_backward/pallas_call | solution.py:245
  105.6 2.3 %fusion = bf16[1280,512]{1,0:T(8,128)(2,1)S(1)} fusion(bf16[4,128,1280]{2,1,0:T(8,128)(2,1)} %get-tuple-element.12, bf16[4,128,512]{2,1,0:T(8,128)(2,1)} %get-tuple-element.13), kind=kOutput, calls=%fused_computation.2 | convolution fusion | flops 671744000 | bytes 3145728 | tf_op jit(solution)/shard_map/dot_general | solution.py:22
  107.9 1.3 reshape.2
  109.2 12.1 %all-to-all-start = ((bf16[64,20,512]{2,1,0:T(8,128)(2,1)}), bf16[64,20,512]{2,1,0:T(8,128)(2,1)S(1)}, u32[]{:S(2)}, u32[]{:S(2)}) async-start(bf16[64,20,512]{2,1,0:T(8,128)(2,1)} %reshape.2), calls=%async_computation | async-start | bytes 3145728 | tf_op jit(solution)/shard_map/all_to_all | solution.py:258
  121.3 0.0 copy-start
  121.3 40.8 %all-to-all-done = bf16[64,20,512]{2,1,0:T(8,128)(2,1)S(1)} async-done(((bf16[64,20,512]{2,1,0:T(8,128)(2,1)}), bf16[64,20,512]{2,1,0:T(8,128)(2,1)S(1)}, u32[]{:S(2)}, u32[]{:S(2)}) %all-to-all-start) | async-done | bytes 1310752 | tf_op jit(solution)/shard_map/all_to_all | solution.py:258
  162.1 0.9 convert_reduce_fusion
  163.0 0.0 copy-done
  163.0 0.0 copy-start.2
  163.0 0.0 copy-start.1
  163.0 1.0 copy.16
  164.0 0.0 copy-done.2
  164.0 0.7 copy.17
  164.7 0.0 copy-done.1
  164.7 0.7 copy.18
Async XLA Ops:
  109.2 52.9 %all-to-all-start = ((bf16[64,20,512]{2,1,0:T(8,128)(2,1)}), bf16[64,20,512]{2,1,0:T(8,128)(2,1)S(1)}, u32[]{:S(2)}, u32[]{:S(2)}) async-start(bf16[64,20,512]{2,1,0:T(8,128)(2,1)} %reshape.2), calls=%async_computation | async-start | bytes 3145728 | tf_op jit(solution)/shard_map/all_to_all | solution.py:258
  121.3 41.7 %copy-start = (bf16[1,128,4096]{2,1,0:T(8,128)(2,1)S(1)}, bf16[1,128,4096]{2,1,0:T(8,128)(2,1)}, u32[]{:S(2)}) copy-start(bf16[1,128,4096]{2,1,0:T(8,128)(2,1)} %get-tuple-element.18) | copy-start | bytes 3145732
  163.0 1.0 copy-start.2
  163.0 1.7 %copy-start.1 = (bf16[1,128,512]{2,1,0:T(8,128)(2,1)S(1)}, bf16[1,128,512]{2,1,0:T(8,128)(2,1)}, u32[]{:S(2)}) copy-start(bf16[1,128,512]{2,1,0:T(8,128)(2,1)} %get-tuple-element.20) | copy-start | bytes 393220

commit v3 on v2

v3 whole, which is shorter than its diff:
```python
import jax
import jax.numpy as jnp
from jax import lax
from jax.sharding import Mesh, PartitionSpec as P
from jax.experimental import pallas as pl
from jax.experimental.pallas import tpu as pltpu

bf = jnp.bfloat16
f32 = jnp.float32
HEADS = 8
D = 128
ROWS = 128
LANES = HEADS * ROWS
SCALE = D ** -0.5
LOG = SCALE * 1.4426950408889634
CHUNK = 512
BLOCKS = CHUNK // ROWS
XCOLS = 1280


def dot(a, b, ca, cb):
    return lax.dot_general(a, b, (((ca,), (cb,)), ((), ())), preferred_element_type=f32)


def cols(index, width):
    return pl.ds(pl.multiple_of(index * width, width), width)


def remote(src, dst, sems, at, peer, there=None):
    return pltpu.make_async_remote_copy(src_ref=src, dst_ref=dst, send_sem=sems[0].at[at],
                                        recv_sem=sems[1].at[at if there is None else there],
                                        device_id=peer, device_id_type=pl.DeviceIdType.MESH)


def arrived(ref, sem):
    pltpu.make_async_copy(ref, ref, sem).wait()


def kernel(q, g, o, k, v, xin, dqo, dko, dvo, wo,
           kv, kt, qr, gr, dr, gl, xl, dl, qt, gt, qn, gn, rs, sh, S, E, dka, dva, dqt, dqv, part, rcv, fin,
           xp, xr, xt, dvall, wb, wrc, w2, wrp, w3, wrh, *sems):
    (lg, lo), sk, sv, sq, sg, sd, sx, sb, sc, sdq, sp, srk, srv, sdv, swc, swp, swh = [
        sems[i:i + 2] for i in range(0, 34, 2)]
    x, z, y, h, c = (lax.axis_index(a) for a in ("x", "z", "y", "h", "c"))
    me = 8 * x + 4 * z + y

    def mod4(i):
        return lax.rem(i + 4, 4)

    xs = [mod4(x + d) for d in range(4)]
    ys = [mod4(y + e) for e in range(4)]
    hs = [mod4(h + e) for e in range(4)]
    near = [(dz, e) for dz in range(2) for e in range(4) if dz or e]

    def in_plane(dz, e):
        return {"z": (1 - z) if dz else z, "y": ys[e]}

    def in_side(dz, d):
        return {"x": xs[d], "z": (1 - z) if dz else z}

    barrier = pltpu.get_barrier_semaphore()
    friends = [{"x": xs[d], "y": ys[e]} for d in range(4) for e in range(4) if d or e]
    friends += [in_plane(1, e) for e in range(4)] + [in_side(1, d) for d in (1, 2, 3)]
    friends += [{"c": 1 - c}] + [{"h": hs[e]} for e in (1, 2, 3)]
    for friend in friends:
        pl.semaphore_signal(barrier, inc=1, device_id=friend, device_id_type=pl.DeviceIdType.MESH)
    get_g = pltpu.make_async_copy(g.at[0], gl, lg)
    get_o = pltpu.make_async_copy(o.at[0], xl.at[:, 0:4 * LANES], lo)
    get_x = pltpu.make_async_copy(xin.at[0], xl, lo)
    get_g.start()
    get_o.start()
    pl.semaphore_wait(barrier, len(friends))

    sends = []

    def send(*a):
        copy = remote(*a)
        copy.start()
        sends.append(copy)

    for src, dst, s, width in ((k.at[0], kv.at[me, :, 0:D], sk, D), (v.at[0], kv.at[me, :, D:2 * D], sv, D),
                               (q.at[0], qr.at[x], sq, LANES), (g.at[0], gr.at[x], sg, LANES)):
        for d in (1, 3, 2):
            send(src.at[:, cols(xs[d], width)], dst, s, d, {"x": xs[d]})
        pltpu.make_async_copy(src.at[:, cols(x, width)], dst, s[1].at[0]).start()

    get_g.wait()
    get_o.wait()
    head = lax.broadcasted_iota(jnp.int32, (HEADS, LANES), 0)
    ones = jnp.where(head == lax.broadcasted_iota(jnp.int32, (HEADS, LANES), 1) // D, 1.0, 0.0).astype(bf)
    for j in range(4):
        at = slice(j * LANES, (j + 1) * LANES)
        prod = gl[:, at].astype(f32) * xl[:, at].astype(f32)
        high = prod.astype(bf)
        low = (prod - high.astype(f32)).astype(bf)
        dl[j] = dot(ones, high, 1, 1) + dot(ones, low, 1, 1)
    get_x.start()
    for d in (1, 3, 2):
        send(dl.at[xs[d]], dr.at[x], sd, d, {"x": xs[d]})
    pltpu.make_async_copy(dl.at[x], dr.at[x], sd[1].at[0]).start()

    def slot(s, zz, yy):
        return kv.at[8 * s + 4 * zz + yy]

    for s in range(4):
        d = mod4(x - s)
        mine = slot(s, z, y)
        arrived(mine.at[:, 0:D], sk[1].at[d])
        arrived(mine.at[:, D:2 * D], sv[1].at[d])
        for e in (1, 3, 2):
            send(mine, mine, sc, (s, e), {"y": ys[e]})
        send(mine, mine, sb, (s, 0), {"z": 1 - z})

    get_x.wait()
    for j in range(4):
        xp[j] = jnp.concatenate([xl[:, 640 * b + 160 * j:640 * b + 160 * j + 160] for b in range(8)], axis=1)
    for e in (1, 3, 2):
        send(xp.at[ys[e]], xr.at[y], sx, e, {"y": ys[e]})
    pltpu.make_async_copy(xp.at[y], xr.at[y], sx[1].at[0]).start()

    dka[...] = jnp.zeros_like(dka)
    dva[...] = jnp.zeros_like(dva)
    dqt[...] = jnp.zeros_like(dqt)

    def relay(s):
        for e in (1, 3, 2):
            theirs = slot(s, z, mod4(y - e))
            arrived(theirs, sc[1].at[s, e])
            remote(theirs, theirs, sb, (s, e), {"z": 1 - z}).start()

    def chunk_of(ch):
        return pl.ds(ch * BLOCKS, BLOCKS)

    def stats(s, carry):
        d = mod4(x - s)
        i = 8 * s + 4 * z + y
        for e in range(4):
            arrived(slot(s, 1 - z, mod4(y - e)), sb[1].at[s, e])
        for b in range(8):
            kt[:, cols(8 * s + b, D)] = kv[8 * s + b, :, 0:D].T
        arrived(qr.at[s], sq[1].at[d])
        arrived(dr.at[s], sd[1].at[d])
        for n in range(HEADS):
            cs = slice(n * D, (n + 1) * D)
            qh = qr[s, :, cs]
            qt[:, cs] = qh.T
            qn[s, cs, :] = qh
        n = i // BLOCKS

        def score(ch):
            return dot(kv[chunk_of(ch), :, 0:D].reshape(CHUNK, D), qt[...], 1, 0)

        def top(m, t):
            return jnp.maximum(m, jnp.max(t.reshape(CHUNK // 8, 8, LANES), axis=0))

        def p1(ch, m):
            t = score(ch)
            S[cols(ch, CHUNK), :] = t
            return top(m, t)

        m = lax.fori_loop(0, n, p1, jnp.full((8, LANES), -1e30, f32))
        last = score(n)
        key = n * CHUNK + lax.broadcasted_iota(jnp.int32, (CHUNK, LANES), 0)
        row = i * ROWS + lax.broadcasted_iota(jnp.int32, (CHUNK, LANES), 1) % ROWS
        last = jnp.where(key <= row, last, -1e30)
        S[cols(n, CHUNK), :] = last
        mc = jnp.max(top(m, last), axis=0, keepdims=True) * LOG

        def p2(ch, total, keep):
            e = jnp.exp2(S[cols(ch, CHUNK), :] * LOG - mc)
            if keep:
                S[cols(ch, CHUNK), :] = e
            else:
                E[cols(s * (s + 1) + ch, CHUNK), :] = e.astype(bf)
            return total + jnp.sum(e.reshape(CHUNK // 8, 8, LANES), axis=0)

        def finish(keep):
            total = lax.fori_loop(0, n + 1, lambda ch, t: p2(ch, t, keep), jnp.zeros((8, LANES), f32))
            r = 1.0 / jnp.sum(total, axis=0, keepdims=True)
            rs[s] = r
            sh[s] = jnp.concatenate([dr[s, a:a + 1, :] for a in range(HEADS)], axis=1) * r

        pl.when(s < 3)(lambda: finish(False))
        pl.when(s == 3)(lambda: finish(True))

        @pl.when(s < 2)
        def _():
            relay(s + 2)

        return carry

    relay(0)
    relay(1)
    lax.fori_loop(0, 4, stats, 0)

    def scale(s, carry):
        arrived(gr.at[s], sg[1].at[mod4(x - s)])
        for n in range(HEADS):
            cs = slice(n * D, (n + 1) * D)
            gh = (gr[s, :, cs].astype(f32).T * rs[s, :, cs]).astype(bf)
            gt[s, :, cs] = gh
            gn[s, cs, :] = gh.T
        return carry

    lax.fori_loop(0, 4, scale, 0)

    def grads(s, ch, e32, e):
        at = cols(ch, CHUNK)
        values = kv[chunk_of(ch), :, D:2 * D].reshape(CHUNK, D)
        ds = (e32 * (dot(values, gt[s], 1, 0) - sh[s])).astype(bf)
        dva[at, :] += dot(e, gn[s], 1, 0)
        dka[at, :] += dot(ds, qn[s], 1, 0)
        dqt[s] += dot(kt[:, at], ds, 1, 0)

    def wide(ch, carry):
        e = S[cols(ch, CHUNK), :]
        grads(3, ch, e, e.astype(bf))
        return carry

    def reduce(s):
        own = 4 * z + y
        total = part[s, own].astype(f32)
        for dz, e in near:
            n = dz * 4 + e
            arrived(rcv.at[n, s], sp[1].at[n, s])
            total = total + rcv[n, s].astype(f32)
        fin[s] = total.astype(bf)

        def deliver(src, dst, s2, at, there, peer, local):
            @pl.when(local)
            def _():
                pltpu.make_async_copy(src, dst, s2[1].at[there]).start()

            @pl.when(jnp.logical_not(local))
            def _():
                remote(src, dst, s2, at, peer, there).start()

        home = s == x
        for e in range(4):
            if e:
                remote(fin.at[s, :, D:2 * D], dvall.at[y, :, cols(x, D)], sdv, (s, e), {"x": s, "y": ys[e]}, (x, y)).start()
            else:
                deliver(fin.at[s, :, D:2 * D], dvall.at[y, :, cols(x, D)], sdv, (s, 0), (x, y), {"x": s}, home)
        deliver(fin.at[s, :, 0:D], dko.at[0, :, cols(x, D)], srk, s, x, {"x": s}, home)
        deliver(fin.at[s, :, D:2 * D], dvo.at[0, :, cols(x, D)], srv, s, x, {"x": s}, home)

    def group(turn, carry):
        a = 3 - turn
        lax.fori_loop(2 * a, jnp.minimum(2 * a + 2, 7 + z), wide, 0)

        def narrow(s, carry):
            def one(ch, carry):
                e = E[cols(s * (s + 1) + ch, CHUNK), :]
                grads(s, ch, e.astype(f32), e)
                return carry

            lax.fori_loop(2 * a, jnp.minimum(2 * a + 2, 2 * s + 1 + z), one, 0)
            return carry

        lax.fori_loop(a, 3, narrow, 0)
        for b in range(8):
            at = pl.ds(pl.multiple_of(a * 1024 + b * ROWS, ROWS), ROWS)
            part[a, b, :, 0:D] = (dka[at, :] * SCALE).astype(bf)
            part[a, b, :, D:2 * D] = dva[at, :].astype(bf)
        for dz, e in near:
            peer = in_plane(dz, e)
            n = dz * 4 + e
            remote(part.at[a, 4 * peer["z"] + peer["y"]], rcv.at[n, a], sp, (n, a), peer).start()

        @pl.when(turn > 0)
        def _():
            reduce(a + 1)

        @pl.when(turn == 1)
        def _():
            line = lax.broadcasted_iota(jnp.int32, (320, 640), 0)
            want = line + 20 * lax.shift_right_logical(line * 3277, 16)
            place = lax.broadcasted_iota(jnp.int32, (320, 640), 1)
            for e in range(4):
                arrived(xr.at[mod4(y - e)], sx[1].at[e])
            for part_c in range(2):
                pick = jnp.where(place == want + 20 * part_c, 1.0, 0.0).astype(bf)
                for half in range(2):
                    for j in range(4):
                        xt[part_c, half * 320:half * 320 + 320, j * ROWS:(j + 1) * ROWS] = dot(
                            pick, xr[j, :, half * 640:half * 640 + 640], 1, 1).astype(bf)

        return carry

    lax.fori_loop(0, 4, group, 0)

    def give_dq(t, carry):
        s = 3 - t
        for n in range(HEADS):
            cs = slice(n * D, (n + 1) * D)
            dqv[s, :, cs] = (dqt[s, :, cs].T * SCALE).astype(bf)
        home = dqo.at[0, :, cols(x, LANES)]

        @pl.when(s == x)
        def _():
            pltpu.make_async_copy(dqv.at[s], home, sdq[1].at[0]).start()

        @pl.when(s != x)
        def _():
            remote(dqv.at[s], home, sdq, mod4(s - x), {"x": s}).start()

        return carry

    lax.fori_loop(0, 4, give_dq, 0)
    reduce(0)

    for j in range(4):
        for b in range(4):
            arrived(dvall.at[b, :, cols(j, D)], sdv[1].at[j, b])
    tall = dvall[...].reshape(4 * ROWS, 4 * D)

    def weigh(part_c):
        for t in range(4):
            at = slice(t * 160, t * 160 + 160)
            wb[part_c, at, :] = dot(xt[part_c, at, :], tall, 1, 0).astype(bf)

    weigh(1 - c)
    send(wb.at[1 - c], wrc, swc, 0, {"c": 1 - c})
    weigh(c)
    arrived(wrc, swc[1].at[0])
    for b in range(8):
        at = slice(b * 80, b * 80 + 80)
        w2[b] = (wb[c, at, :].astype(f32) + wrc[at, :].astype(f32)).astype(bf)
    for dz, d in near:
        peer = in_side(dz, d)
        send(w2.at[2 * peer["x"] + peer["z"]], wrp.at[dz * 4 + d], swp, dz * 4 + d, peer)
    total = w2[2 * x + z].astype(f32)
    for dz, d in near:
        n = dz * 4 + d
        arrived(wrp.at[n], swp[1].at[n])
        total = total + wrp[n].astype(f32)
    for e in range(4):
        w3[e] = jnp.concatenate([total[20 * e:20 * e + 20], jnp.zeros((12, 4 * D), f32)], axis=0).astype(bf)
    for e in (1, 3, 2):
        send(w3.at[hs[e]], wrh.at[e], swh, e, {"h": hs[e]})
    last = w3[h].astype(f32)
    for e in (1, 3, 2):
        arrived(wrh.at[e], swh[1].at[e])
        last = last + wrh[e].astype(f32)
    wo[...] = last[0:20]

    for d in range(4):
        f = mod4(x - d)
        arrived(dqo.at[0, :, cols(f, LANES)], sdq[1].at[d])
        arrived(dko.at[0, :, cols(d, D)], srk[1].at[d])
        arrived(dvo.at[0, :, cols(d, D)], srv[1].at[d])
    for copy in sends:
        copy.wait_send()
    for s in range(4):
        for e in (1, 2, 3):
            theirs = slot(s, z, mod4(y - e))
            remote(theirs, theirs, sb, (s, e), {"z": 1 - z}).wait_send()
    for d in (1, 2, 3):
        remote(dqv.at[xs[d]], dqo.at[0, :, cols(x, LANES)], sdq, d, {"x": xs[d]}).wait_send()
    for dz, e in near:
        n = dz * 4 + e
        for a in range(4):
            remote(part.at[a, 0], rcv.at[n, a], sp, (n, a), in_plane(dz, e)).wait_send()
    for s in range(4):
        for e in (1, 2, 3):
            remote(fin.at[s, :, D:2 * D], dvall.at[y, :, cols(x, D)], sdv, (s, e), {"y": ys[e]}).wait_send()
    for d in (1, 2, 3):
        t = xs[d]
        remote(fin.at[t, :, D:2 * D], dvall.at[y, :, cols(x, D)], sdv, (t, 0), {"x": t}).wait_send()
        remote(fin.at[t, :, 0:D], dko.at[0, :, cols(x, D)], srk, t, {"x": t}).wait_send()
        remote(fin.at[t, :, D:2 * D], dvo.at[0, :, cols(x, D)], srv, t, {"x": t}).wait_send()


def per_device(x_in, q, k, v, o, g):
    T = 32 * ROWS
    anyspace = pl.BlockSpec(memory_space=pl.ANY)
    sems = [(), ()] + [(4,)] * 12 + [(4, 4)] * 4 + [(4,)] * 2 + [(8, 4)] * 2 + [(4,)] * 4 + [(4, 4)] * 2 + [(1,)] * 2
    sems += [(8,)] * 2 + [(4,)] * 2
    wide, tall = (ROWS, 4 * LANES), (T, D)
    scratch = [((32, ROWS, 2 * D), bf), ((D, T), bf), ((4, ROWS, LANES), bf), ((4, ROWS, LANES), bf), ((4, HEADS, ROWS), f32),
               (wide, bf), ((ROWS, 4 * XCOLS), bf), ((4, HEADS, ROWS), f32), ((D, LANES), bf), ((4, D, LANES), bf),
               ((4, LANES, D), bf), ((4, LANES, D), bf), ((4, 1, LANES), f32), ((4, 1, LANES), f32),
               ((T, LANES), f32), ((12 * CHUNK, LANES), bf), (tall, f32), (tall, f32), ((4, D, LANES), f32),
               ((4, ROWS, LANES), bf), ((4, 8, ROWS, 2 * D), bf), ((8, 4, ROWS, 2 * D), bf), ((4, ROWS, 2 * D), bf),
               ((4, ROWS, XCOLS), bf), ((4, ROWS, XCOLS), bf), ((2, XCOLS // 2, 4 * ROWS), bf), ((4, ROWS, 4 * D), bf),
               ((2, XCOLS // 2, 4 * D), bf), ((XCOLS // 2, 4 * D), bf), ((8, 80, 4 * D), bf), ((8, 80, 4 * D), bf),
               ((4, 32, 4 * D), bf), ((4, 32, 4 * D), bf)]
    return pl.pallas_call(
        kernel,
        out_shape=[jax.ShapeDtypeStruct((1, ROWS, 4 * LANES), bf), jax.ShapeDtypeStruct((1, ROWS, 4 * D), bf),
                   jax.ShapeDtypeStruct((1, ROWS, 4 * D), bf), jax.ShapeDtypeStruct((20, 4 * D), f32)],
        in_specs=[anyspace] * 6,
        out_specs=[anyspace] * 3 + [pl.BlockSpec(memory_space=pltpu.VMEM)],
        scratch_shapes=[pltpu.VMEM(*s) for s in scratch] + [pltpu.SemaphoreType.DMA(s) for s in sems],
        compiler_params=pltpu.CompilerParams(vmem_limit_bytes=62 << 20, collective_id=0, has_side_effects=True),
        name="attention_backward")(q, g, o, k, v, x_in)


def solution(mesh):
    fine = Mesh(mesh.devices.reshape(4, 2, 4, 4, 2), ("x", "z", "y", "h", "c"))
    seq, dp = ("x", "z", "y"), ("h", "c")
    rows = P(dp, seq, None)
    return jax.shard_map(per_device, mesh=fine, in_specs=(rows,) * 6,
                         out_specs=(rows, rows, rows, P(seq + dp, None)), check_vma=False)
```

time: 167 us -> 134 us (0.80)
  waiting for transfers between devices: 40.8 us -> 0 us
  Pallas kernels: 105 us -> 128 us
  starting transfers between devices: 12.1 us -> 0 us
  matrix products: 2.31 us -> 0 us
    all_to_all x1 -> x0, waiting for transfers between devices: 40.8 us -> none  [per_device(): lax.all_to_all(w.reshape(64, -1, 4 * D), ('z', 'y', 'h', 'c'), 0, 0, tile...]
    pallas_call x1, Pallas kernels: 105 us -> 128 us  [per_device(): pl.pallas_call(kernel, out_shape=[jax.ShapeDtypeStruct((1, ROWS, 4 * LANE...]
    all_to_all x1 -> x0, starting transfers between devices: 12.1 us -> none  [per_device(): lax.all_to_all(w.reshape(64, -1, 4 * D), ('z', 'y', 'h', 'c'), 0, 0, tile...]
    dot_general x1 -> x0, matrix products: 2.31 us -> none  [dot(): lax.dot_general(a, b, (((ca,), (cb,)), ((), ())), preferred_element_type=...]
    unnamed x9 -> x10, local copies, waits for them, and re-layouts: 2.31 us -> 4.27 us
  transfers between devices with their start and end apart: 1 -> 0, of which waited for: 1 -> 0; matrix products, arithmetic and copies ran while one was open for 0% -> 0% of each run, Pallas kernels for 0% -> 0%
where the time goes in v3:
time: 134 us; the launch traced here: 133 us
  Pallas kernels  128 us (96%)
  local copies, waits for them, and re-layouts  4.27 us (3%)
    pallas_call x1, Pallas kernels, per_device(): pl.pallas_call(kernel, out_shape=[jax.ShapeDtypeStruct((1, ROWS, 4 * LANE...  128 us
    unnamed x10, local copies, waits for them, and re-layouts  4.27 us

profile of v3, /device:TPU:6, one launch (start us, length us, event | category | flops | bytes accessed | tf_op | source)
XLA Modules:
  0.0 133.3 jit_solution(17338735864194850826)
XLA Ops:
  0.6 128.4 %attention_backward.1 = (bf16[1,128,4096]{2,1,0:T(8,128)(2,1)}, bf16[1,128,512]{2,1,0:T(8,128)(2,1)}, bf16[1,128,512]{2,1,0:T(8,128)(2,1)}, f32[20,512]{1,0:T(8,128)}) custom-call(bf16[1,128,4096]{2,1,0:T(8,128)(2,1)} %q.1, bf16[1,128,4096]{2,1,0:T(8,128)(2,1)} %g.1, bf16[1,128,4096]{2,1,0:T(8,128)(2,1)} %o.1, bf16[1,128,512]{2,1,0:T(8,128)(2,1)} %k.1, ...), custom_call_target="tpu_custom_call" | custom-call | tf_op jit(solution)/shard_map/attention_backward/pallas_call | solution.py:388
  129.0 0.0 copy-start.1
  129.0 0.0 copy-start
  129.0 0.0 copy-start.2
  129.0 2.3 %copy.14 = bf16[1,128,4096]{2,1,0:T(8,128)(2,1)} copy(bf16[1,128,4096]{2,1,0:T(8,128)(2,1)} %get-tuple-element.8) | data formatting | bytes 2097152
  131.4 0.0 copy-done.1
  131.4 0.7 copy.15
  132.0 0.0 copy-done
  132.0 0.7 copy.16
  132.7 0.0 copy-done.2
  132.7 0.6 copy.17
Async XLA Ops:
  129.0 2.4 %copy-start.1 = (bf16[1,128,512]{2,1,0:T(8,128)(2,1)S(1)}, bf16[1,128,512]{2,1,0:T(8,128)(2,1)}, u32[]{:S(2)}) copy-start(bf16[1,128,512]{2,1,0:T(8,128)(2,1)} %get-tuple-element.9) | copy-start | bytes 393220
  129.0 3.0 %copy-start = (bf16[1,128,512]{2,1,0:T(8,128)(2,1)S(1)}, bf16[1,128,512]{2,1,0:T(8,128)(2,1)}, u32[]{:S(2)}) copy-start(bf16[1,128,512]{2,1,0:T(8,128)(2,1)} %get-tuple-element.10) | copy-start | bytes 393220
  129.0 3.7 %copy-start.2 = (f32[20,512]{1,0:T(8,128)S(1)}, f32[20,512]{1,0:T(8,128)}, u32[]{:S(2)}) copy-start(f32[20,512]{1,0:T(8,128)} %get-tuple-element.11) | copy-start | bytes 122884

commit v4 on v3

v4 whole, which is shorter than its diff:
```python
import jax
import jax.numpy as jnp
from jax import lax
from jax.sharding import Mesh, PartitionSpec as P
from jax.experimental import pallas as pl
from jax.experimental.pallas import tpu as pltpu

bf = jnp.bfloat16
f32 = jnp.float32
HEADS = 8
D = 128
ROWS = 128
LANES = HEADS * ROWS
SCALE = D ** -0.5
LOG = SCALE * 1.4426950408889634
CHUNK = 512
BLOCKS = CHUNK // ROWS
XCOLS = 1280


def dot(a, b, ca, cb):
    return lax.dot_general(a, b, (((ca,), (cb,)), ((), ())), preferred_element_type=f32)


def cols(index, width):
    return pl.ds(pl.multiple_of(index * width, width), width)


def remote(src, dst, sems, at, peer, there=None):
    return pltpu.make_async_remote_copy(src_ref=src, dst_ref=dst, send_sem=sems[0].at[at],
                                        recv_sem=sems[1].at[at if there is None else there],
                                        device_id=peer, device_id_type=pl.DeviceIdType.MESH)


def arrived(ref, sem):
    pltpu.make_async_copy(ref, ref, sem).wait()


def kernel(q, g, o, k, v, xin, dqo, dko, dvo, wo,
           kv, kt, qr, gr, dr, gl, xl, dl, qn, gn, rs, sh, S, E, dka, dva, dqt, dqv, partk, partv, rcvk, rcvv, fink, finv,
           xp, xr, xt, dvall, wb, wrc, w2, wrp, w3, wrh, *sems):
    (lg, lo), sk, sv, sq, sg, sd, sx, sb, sc, sc2, sdq, spk, spv, srk, srv, sdv, swc, swp, swh = [
        sems[i:i + 2] for i in range(0, 38, 2)]
    x, z, y, h, c = (lax.axis_index(a) for a in ("x", "z", "y", "h", "c"))
    me = 8 * x + 4 * z + y

    def mod4(i):
        return lax.rem(i + 4, 4)

    xs = [mod4(x + d) for d in range(4)]
    ys = [mod4(y + e) for e in range(4)]
    hs = [mod4(h + e) for e in range(4)]
    near = [(dz, e) for dz in range(2) for e in range(4) if dz or e]

    def in_plane(dz, e):
        return {"z": (1 - z) if dz else z, "y": ys[e]}

    def in_side(dz, d):
        return {"x": xs[d], "z": (1 - z) if dz else z}

    barrier = pltpu.get_barrier_semaphore()
    friends = [{"x": xs[d], "y": ys[e]} for d in range(4) for e in range(4) if d or e]
    friends += [in_plane(1, e) for e in range(4)] + [in_side(1, d) for d in (1, 2, 3)]
    friends += [{"c": 1 - c}] + [{"h": hs[e]} for e in (1, 2, 3)]
    for friend in friends:
        pl.semaphore_signal(barrier, inc=1, device_id=friend, device_id_type=pl.DeviceIdType.MESH)
    get_g = pltpu.make_async_copy(g.at[0], gl, lg)
    get_o = pltpu.make_async_copy(o.at[0], xl.at[:, 0:4 * LANES], lo)
    get_x = pltpu.make_async_copy(xin.at[0], xl, lo)
    get_g.start()
    get_o.start()
    pl.semaphore_wait(barrier, len(friends))

    sends = []

    def send(*a):
        copy = remote(*a)
        copy.start()
        sends.append(copy)

    def spread(src, dst, s, width, which):
        for d in which:
            send(src.at[0, :, cols(xs[d], width)], dst, s, d, {"x": xs[d]})

    def stay(src, dst, s, width):
        pltpu.make_async_copy(src.at[0, :, cols(x, width)], dst, s[1].at[0]).start()

    spread(k, kv.at[me, :, 0:D], sk, D, (1, 3, 2))
    spread(v, kv.at[me, :, D:2 * D], sv, D, (1, 3, 2))
    stay(k, kv.at[me, :, 0:D], sk, D)
    stay(v, kv.at[me, :, D:2 * D], sv, D)
    spread(q, qr.at[x], sq, LANES, (1, 3))
    stay(q, qr.at[x], sq, LANES)
    stay(g, gr.at[x], sg, LANES)

    get_g.wait()
    get_o.wait()
    head = lax.broadcasted_iota(jnp.int32, (HEADS, LANES), 0)
    ones = jnp.where(head == lax.broadcasted_iota(jnp.int32, (HEADS, LANES), 1) // D, 1.0, 0.0).astype(bf)
    for j in range(4):
        at = slice(j * LANES, (j + 1) * LANES)
        prod = gl[:, at].astype(f32) * xl[:, at].astype(f32)
        high = prod.astype(bf)
        low = (prod - high.astype(f32)).astype(bf)
        dl[j] = dot(ones, high, 1, 1) + dot(ones, low, 1, 1)
    get_x.start()
    for d in (1, 3, 2):
        send(dl.at[xs[d]], dr.at[x], sd, d, {"x": xs[d]})
    pltpu.make_async_copy(dl.at[x], dr.at[x], sd[1].at[0]).start()

    def slot(s, zz, yy):
        return kv.at[8 * s + 4 * zz + yy]

    for s in range(4):
        d = mod4(x - s)
        mine = slot(s, z, y)
        arrived(mine.at[:, 0:D], sk[1].at[d])
        arrived(mine.at[:, D:2 * D], sv[1].at[d])
        send(mine, mine, sb, (s, 0), {"z": 1 - z})
        for e in (1, 3, 2):
            send(mine, mine, sc, (s, e), {"y": ys[e]})

    spread(q, qr.at[x], sq, LANES, (2,))
    spread(g, gr.at[x], sg, LANES, (1, 3))

    get_x.wait()
    for j in range(4):
        xp[j] = jnp.concatenate([xl[:, 640 * b + 160 * j:640 * b + 160 * j + 160] for b in range(8)], axis=1)
    dka[...] = jnp.zeros_like(dka)
    dqt[...] = jnp.zeros_like(dqt)

    for s in (0, 1):
        theirs = slot(s + 2, 1 - z, y)
        arrived(theirs, sb[1].at[s + 2, 0])
        for e in (1, 3, 2):
            send(theirs, theirs, sc2, (s + 2, e), {"y": ys[e]})
        for e in (1, 3, 2):
            theirs = slot(s, z, mod4(y - e))
            arrived(theirs, sc[1].at[s, e])
            send(theirs, theirs, sb, (s, e), {"z": 1 - z})
    spread(g, gr.at[x], sg, LANES, (2,))
    for e in (1, 3, 2):
        send(xp.at[ys[e]], xr.at[y], sx, e, {"y": ys[e]})
    pltpu.make_async_copy(xp.at[y], xr.at[y], sx[1].at[0]).start()

    def chunk_of(ch):
        return pl.ds(ch * BLOCKS, BLOCKS)

    def stats(s, carry):
        d = mod4(x - s)
        i = 8 * s + 4 * z + y

        @pl.when(s < 2)
        def _():
            for e in range(4):
                arrived(slot(s, 1 - z, mod4(y - e)), sb[1].at[s, e])

        @pl.when(s >= 2)
        def _():
            for e in (1, 2, 3):
                arrived(slot(s, z, mod4(y - e)), sc[1].at[s, e])
                arrived(slot(s, 1 - z, mod4(y - e)), sc2[1].at[s, e])

        for b in range(8):
            kt[:, cols(8 * s + b, D)] = kv[8 * s + b, :, 0:D].T
        arrived(qr.at[s], sq[1].at[d])
        arrived(dr.at[s], sd[1].at[d])
        for n in range(HEADS):
            cs = slice(n * D, (n + 1) * D)
            qn[s, cs, :] = qr[s, :, cs]
        n = i // BLOCKS

        def score(ch):
            return dot(kv[chunk_of(ch), :, 0:D].reshape(CHUNK, D), qn[s], 1, 1)

        def top(m, t):
            return jnp.maximum(m, jnp.max(t.reshape(CHUNK // 8, 8, LANES), axis=0))

        def p1(ch, m):
            t = score(ch)
            S[cols(ch, CHUNK), :] = t
            return top(m, t)

        m = lax.fori_loop(0, n, p1, jnp.full((8, LANES), -1e30, f32))
        last = score(n)
        key = n * CHUNK + lax.broadcasted_iota(jnp.int32, (CHUNK, LANES), 0)
        row = i * ROWS + lax.broadcasted_iota(jnp.int32, (CHUNK, LANES), 1) % ROWS
        last = jnp.where(key <= row, last, -1e30)
        S[cols(n, CHUNK), :] = last
        mc = jnp.max(top(m, last), axis=0, keepdims=True) * LOG

        def p2(ch, total, keep):
            e = jnp.exp2(S[cols(ch, CHUNK), :] * LOG - mc)
            if keep:
                S[cols(ch, CHUNK), :] = e
            else:
                E[cols(s * (s + 1) + ch, CHUNK), :] = e.astype(bf)
            return total + jnp.sum(e.reshape(CHUNK // 8, 8, LANES), axis=0)

        def finish(keep):
            total = lax.fori_loop(0, n + 1, lambda ch, t: p2(ch, t, keep), jnp.zeros((8, LANES), f32))
            r = 1.0 / jnp.sum(total, axis=0, keepdims=True)
            rs[s] = r
            sh[s] = jnp.concatenate([dr[s, a:a + 1, :] for a in range(HEADS)], axis=1) * r

        pl.when(s < 3)(lambda: finish(False))
        pl.when(s == 3)(lambda: finish(True))

        return carry

    lax.fori_loop(0, 4, stats, 0)

    def scale(s, carry):
        arrived(gr.at[s], sg[1].at[mod4(x - s)])
        heads = jnp.concatenate([rs[s, :, n * D:(n + 1) * D] for n in range(HEADS)], axis=0).T
        for n in range(HEADS):
            cs = slice(n * D, (n + 1) * D)
            gn[s, cs, :] = (gr[s, :, cs].astype(f32) * heads[:, n:n + 1]).astype(bf)
        return carry

    def grads(s, ch, e32):
        at = cols(ch, CHUNK)
        values = kv[chunk_of(ch), :, D:2 * D].reshape(CHUNK, D)
        ds = (e32 * (dot(values, gn[s], 1, 1) - sh[s])).astype(bf)
        dka[at, :] += dot(ds, qn[s], 1, 0)
        dqt[s] += dot(kt[:, at], ds, 1, 0)

    def wide(ch, carry):
        grads(3, ch, S[cols(ch, CHUNK), :])
        return carry

    def narrow(s, first, end):
        def one(ch, carry):
            grads(s, ch, E[cols(s * (s + 1) + ch, CHUNK), :].astype(f32))
            return carry

        lax.fori_loop(first, end, one, 0)

    def give_dq(s):
        for n in range(HEADS):
            cs = slice(n * D, (n + 1) * D)
            dqv[s, :, cs] = (dqt[s, :, cs] * SCALE).astype(bf).T
        home = dqo.at[0, :, cols(x, LANES)]

        @pl.when(s == x)
        def _():
            pltpu.make_async_copy(dqv.at[s], home, sdq[1].at[0]).start()

        @pl.when(s != x)
        def _():
            remote(dqv.at[s], home, sdq, mod4(s - x), {"x": s}).start()

    def total_of(part, rcv, sems, s):
        total = part[s, 4 * z + y].astype(f32)
        for dz, e in near:
            n = dz * 4 + e
            arrived(rcv.at[n, s], sems[1].at[n, s])
            total = total + rcv[n, s].astype(f32)
        return total.astype(bf)

    def deliver(src, dst, s2, at, there, s):
        @pl.when(s == x)
        def _():
            pltpu.make_async_copy(src, dst, s2[1].at[there]).start()

        @pl.when(s != x)
        def _():
            remote(src, dst, s2, at, {"x": s}, there).start()

    def reduce_v(s, carry):
        finv[s] = total_of(partv, rcvv, spv, s)
        place = dvall.at[y, :, cols(x, D)]
        for e in (1, 3, 2):
            remote(finv.at[s], place, sdv, (s, e), {"x": s, "y": ys[e]}, (x, y)).start()
        deliver(finv.at[s], place, sdv, (s, 0), (x, y), s)
        deliver(finv.at[s], dvo.at[0, :, cols(x, D)], srv, s, x, s)
        return carry

    def reduce_k(s):
        fink[s] = total_of(partk, rcvk, spk, s)
        deliver(fink.at[s], dko.at[0, :, cols(x, D)], srk, s, x, s)

    def hand_out(part, rcv, sems, a, zz):
        dz = lax.rem(z + zz, 2)
        for e in range(4):
            n = dz * 4 + e

            @pl.when(n > 0)
            def _():
                remote(part.at[a, 4 * zz + ys[e]], rcv.at[n, a], sems, (n, a), {"z": zz, "y": ys[e]}).start()

    def values_of(a):
        def one(i, carry):
            zz = 1 - i
            ch = 2 * a + zz

            def share(s):
                e = S[cols(ch, CHUNK), :].astype(bf) if s == 3 else E[cols(s * (s + 1) + ch, CHUNK), :]
                return dot(e, gn[s], 1, 0)

            dva[...] = sum([share(s) for s in range(a + 1, 4)], jnp.zeros((CHUNK, D), f32))

            @pl.when(zz <= z)
            def _():
                dva[...] += share(a)

            for b in range(4):
                partv[a, 4 * zz + b] = dva[b * ROWS:(b + 1) * ROWS, :].astype(bf)
            hand_out(partv, rcvv, spv, a, zz)
            return carry

        lax.fori_loop(0, 2, one, 0)

    order = [(1, 2), (1, 1), (1, 3), (0, 2), (0, 1), (0, 3), (1, 0), (0, 0)]

    def piece(dz, d):
        peer = in_side(dz, d)
        return peer, 2 * peer["x"] + peer["z"]

    def turn_x():
        line = lax.broadcasted_iota(jnp.int32, (320, 640), 0)
        want = line + 20 * lax.shift_right_logical(line * 3277, 16)
        place = lax.broadcasted_iota(jnp.int32, (320, 640), 1)
        for e in range(4):
            arrived(xr.at[mod4(y - e)], sx[1].at[e])
        for part_c in range(2):
            pick = jnp.where(place == want + 20 * part_c, 1.0, 0.0).astype(bf)
            for half in range(2):
                for j in range(4):
                    rows = dot(pick, xr[j, :, half * 640:half * 640 + 640], 1, 1).astype(bf)
                    xt[part_c, half * 4:half * 4 + 4, :, j * ROWS:(j + 1) * ROWS] = rows.reshape(4, 80, ROWS)


    def weigh():
        for j in range(4):
            for b in range(4):
                arrived(dvall.at[b, :, cols(j, D)], sdv[1].at[j, b])
        tall = dvall[...].reshape(4 * ROWS, 4 * D)

        def product(half):
            wb[half] = dot(xt[half].reshape(640, 4 * ROWS), tall, 1, 0).astype(bf).reshape(8, 80, 4 * D)

        product(1 - c)
        for n, (dz, d) in enumerate(order):
            b = piece(dz, d)[1]
            remote(wb.at[1 - c, b], wrc.at[b], swc, n, {"c": 1 - c}).start()
        product(c)

    def over_sides():
        for n, (dz, d) in enumerate(order):
            peer, b = piece(dz, d)
            arrived(wrc.at[b], swc[1].at[n])
            w2[b] = (wb[c, b].astype(f32) + wrc[b].astype(f32)).astype(bf)
            if dz or d:
                remote(w2.at[b], wrp.at[dz * 4 + d], swp, dz * 4 + d, peer).start()

    def over_rest():
        total = w2[2 * x + z].astype(f32)
        for dz, d in near:
            n = dz * 4 + d
            arrived(wrp.at[n], swp[1].at[n])
            total = total + wrp[n].astype(f32)
        for e in range(4):
            w3[e] = jnp.concatenate([total[20 * e:20 * e + 20], jnp.zeros((12, 4 * D), f32)], axis=0).astype(bf)
        for e in (1, 3, 2):
            remote(w3.at[hs[e]], wrh.at[e], swh, e, {"h": hs[e]}).start()

    def step(t, carry):
        ch = 7 - t
        a = ch // 2
        zz = ch - 2 * a
        lax.fori_loop(ch, jnp.minimum(ch + 1, 7 + z), wide, 0)

        narrow(2, ch, jnp.minimum(ch + 1, 5 + z))
        for b in range(4):
            at = pl.ds(pl.multiple_of(ch * CHUNK + b * ROWS, ROWS), ROWS)
            partk[a, 4 * zz + b] = (dka[at, :] * SCALE).astype(bf)
        hand_out(partk, rcvk, spk, a, zz)

        @pl.when(jnp.logical_and(t > 1, zz == z))
        def _():
            reduce_k(a + 1)

        pl.when(t == 1)(weigh)
        pl.when(t == 3)(over_sides)
        pl.when(t == 5)(over_rest)
        return carry

    lax.fori_loop(0, 4, scale, 0)
    for a in (3, 2, 1, 0):
        values_of(a)

    def early(s, carry):
        narrow(s, 0, 2 * s + 1 + z)
        give_dq(s)
        return carry

    lax.fori_loop(0, 2, early, 0)
    lax.fori_loop(0, 4, reduce_v, 0)
    turn_x()
    lax.fori_loop(0, 8, step, 0)
    lax.fori_loop(2, 4, lambda s, carry: (give_dq(s), carry)[1], 0)
    last = w3[h].astype(f32)
    for e in (1, 3, 2):
        arrived(wrh.at[e], swh[1].at[e])
        last = last + wrh[e].astype(f32)
    wo[...] = last[0:20]
    reduce_k(0)

    for d in range(4):
        f = mod4(x - d)
        arrived(dqo.at[0, :, cols(f, LANES)], sdq[1].at[d])
        arrived(dko.at[0, :, cols(d, D)], srk[1].at[d])
        arrived(dvo.at[0, :, cols(d, D)], srv[1].at[d])
    for copy in sends:
        copy.wait_send()
    for d in (1, 2, 3):
        remote(dqv.at[xs[d]], dqo.at[0, :, cols(x, LANES)], sdq, d, {"x": xs[d]}).wait_send()
    for dz, e in near:
        n = dz * 4 + e
        for a in range(4):
            remote(partk.at[a, 0], rcvk.at[n, a], spk, (n, a), in_plane(dz, e)).wait_send()
            remote(partv.at[a, 0], rcvv.at[n, a], spv, (n, a), in_plane(dz, e)).wait_send()
    for s in range(4):
        for e in (1, 2, 3):
            remote(finv.at[s], dvall.at[y, :, cols(x, D)], sdv, (s, e), {"y": ys[e]}).wait_send()
    for d in (1, 2, 3):
        t = xs[d]
        remote(finv.at[t], dvall.at[y, :, cols(x, D)], sdv, (t, 0), {"x": t}).wait_send()
        remote(fink.at[t], dko.at[0, :, cols(x, D)], srk, t, {"x": t}).wait_send()
        remote(finv.at[t], dvo.at[0, :, cols(x, D)], srv, t, {"x": t}).wait_send()
    for n, (dz, d) in enumerate(order):
        peer, b = piece(dz, d)
        remote(wb.at[1 - c, b], wrc.at[b], swc, n, {"c": 1 - c}).wait_send()
        if dz or d:
            remote(w2.at[b], wrp.at[dz * 4 + d], swp, dz * 4 + d, peer).wait_send()
    for e in (1, 2, 3):
        remote(w3.at[hs[e]], wrh.at[e], swh, e, {"h": hs[e]}).wait_send()


def per_device(x_in, q, k, v, o, g):
    T = 32 * ROWS
    anyspace = pl.BlockSpec(memory_space=pl.ANY)
    sems = [(), ()] + [(4,)] * 12 + [(4, 4)] * 6 + [(4,)] * 2 + [(8, 4)] * 4 + [(4,)] * 4 + [(4, 4)] * 2 + [(8,)] * 2
    sems += [(8,)] * 2 + [(4,)] * 2
    wide, tall = (ROWS, 4 * LANES), (T, D)
    scratch = [((32, ROWS, 2 * D), bf), ((D, T), bf), ((4, ROWS, LANES), bf), ((4, ROWS, LANES), bf), ((4, HEADS, ROWS), f32),
               (wide, bf), ((ROWS, 4 * XCOLS), bf), ((4, HEADS, ROWS), f32),
               ((4, LANES, D), bf), ((4, LANES, D), bf), ((4, 1, LANES), f32), ((4, 1, LANES), f32),
               ((T, LANES), f32), ((12 * CHUNK, LANES), bf), (tall, f32), ((CHUNK, D), f32), ((4, D, LANES), f32),
               ((4, ROWS, LANES), bf), ((4, 8, ROWS, D), bf), ((4, 8, ROWS, D), bf), ((8, 4, ROWS, D), bf),
               ((8, 4, ROWS, D), bf), ((4, ROWS, D), bf), ((4, ROWS, D), bf),
               ((4, ROWS, XCOLS), bf), ((4, ROWS, XCOLS), bf), ((2, 8, 80, 4 * ROWS), bf), ((4, ROWS, 4 * D), bf),
               ((2, 8, 80, 4 * D), bf), ((8, 80, 4 * D), bf), ((8, 80, 4 * D), bf), ((8, 80, 4 * D), bf),
               ((4, 32, 4 * D), bf), ((4, 32, 4 * D), bf)]
    return pl.pallas_call(
        kernel,
        out_shape=[jax.ShapeDtypeStruct((1, ROWS, 4 * LANES), bf), jax.ShapeDtypeStruct((1, ROWS, 4 * D), bf),
                   jax.ShapeDtypeStruct((1, ROWS, 4 * D), bf), jax.ShapeDtypeStruct((20, 4 * D), f32)],
        in_specs=[anyspace] * 6,
        out_specs=[anyspace] * 3 + [pl.BlockSpec(memory_space=pltpu.VMEM)],
        scratch_shapes=[pltpu.VMEM(*s) for s in scratch] + [pltpu.SemaphoreType.DMA(s) for s in sems],
        compiler_params=pltpu.CompilerParams(vmem_limit_bytes=62 << 20, collective_id=0, has_side_effects=True),
        name="attention_backward")(q, g, o, k, v, x_in)


def solution(mesh):
    fine = Mesh(mesh.devices.reshape(4, 2, 4, 4, 2), ("x", "z", "y", "h", "c"))
    seq, dp = ("x", "z", "y"), ("h", "c")
    rows = P(dp, seq, None)
    return jax.shard_map(per_device, mesh=fine, in_specs=(rows,) * 6,
                         out_specs=(rows, rows, rows, P(seq + dp, None)), check_vma=False)
```

time: 134 us -> 119 us (0.89)
  Pallas kernels: 128 us -> 114 us
    pallas_call x1, Pallas kernels: 128 us -> 114 us  [per_device(): pl.pallas_call(kernel, out_shape=[jax.ShapeDtypeStruct((1, ROWS, 4 * LANE...]
where the time goes in v4:
time: 119 us
  Pallas kernels  114 us (96%)
  local copies, waits for them, and re-layouts  4.27 us (4%)
    pallas_call x1, Pallas kernels, per_device(): pl.pallas_call(kernel, out_shape=[jax.ShapeDtypeStruct((1, ROWS, 4 * LANE...  114 us
    unnamed x10, local copies, waits for them, and re-layouts  4.27 us

profile of v4, /device:TPU:6, one launch (start us, length us, event | category | flops | bytes accessed | tf_op | source)
XLA Modules:
  0.0 118.7 jit_solution(18062568304015575380)
XLA Ops:
  0.6 113.7 %attention_backward.1 = (bf16[1,128,4096]{2,1,0:T(8,128)(2,1)}, bf16[1,128,512]{2,1,0:T(8,128)(2,1)}, bf16[1,128,512]{2,1,0:T(8,128)(2,1)}, f32[20,512]{1,0:T(8,128)}) custom-call(bf16[1,128,4096]{2,1,0:T(8,128)(2,1)} %q.1, bf16[1,128,4096]{2,1,0:T(8,128)(2,1)} %g.1, bf16[1,128,4096]{2,1,0:T(8,128)(2,1)} %o.1, bf16[1,128,512]{2,1,0:T(8,128)(2,1)} %k.1, ...), custom_call_target="tpu_custom_call" | custom-call | tf_op jit(solution)/shard_map/attention_backward/pallas_call | solution.py:456
  114.4 0.0 copy-start.1
  114.4 0.0 copy-start
  114.4 0.0 copy-start.2
  114.4 2.3 %copy.14 = bf16[1,128,4096]{2,1,0:T(8,128)(2,1)} copy(bf16[1,128,4096]{2,1,0:T(8,128)(2,1)} %get-tuple-element.8) | data formatting | bytes 2097152
  116.7 0.0 copy-done.1
  116.7 0.7 copy.15
  117.4 0.0 copy-done
  117.4 0.7 copy.16
  118.0 0.0 copy-done.2
  118.0 0.6 copy.17
Async XLA Ops:
  114.4 2.4 %copy-start.1 = (bf16[1,128,512]{2,1,0:T(8,128)(2,1)S(1)}, bf16[1,128,512]{2,1,0:T(8,128)(2,1)}, u32[]{:S(2)}) copy-start(bf16[1,128,512]{2,1,0:T(8,128)(2,1)} %get-tuple-element.9) | copy-start | bytes 393220
  114.4 3.0 %copy-start = (bf16[1,128,512]{2,1,0:T(8,128)(2,1)S(1)}, bf16[1,128,512]{2,1,0:T(8,128)(2,1)}, u32[]{:S(2)}) copy-start(bf16[1,128,512]{2,1,0:T(8,128)(2,1)} %get-tuple-element.10) | copy-start | bytes 393220
  114.4 3.7 %copy-start.2 = (f32[20,512]{1,0:T(8,128)S(1)}, f32[20,512]{1,0:T(8,128)}, u32[]{:S(2)}) copy-start(f32[20,512]{1,0:T(8,128)} %get-tuple-element.11) | copy-start | bytes 122884

commit v5 on v4

v5 whole, which is shorter than its diff:
```python
import jax
import jax.numpy as jnp
from jax import lax
from jax.sharding import Mesh, PartitionSpec as P
from jax.experimental import pallas as pl
from jax.experimental.pallas import tpu as pltpu

bf = jnp.bfloat16
f32 = jnp.float32
HEADS = 8
D = 128
ROWS = 128
LANES = HEADS * ROWS
HALF = LANES // 2
SCALE = D ** -0.5
LOG = SCALE * 1.4426950408889634
CHUNK = 512
BLOCKS = CHUNK // ROWS
XCOLS = 1280


def dot(a, b, ca, cb):
    return lax.dot_general(a, b, (((ca,), (cb,)), ((), ())), preferred_element_type=f32)


def cols(index, width):
    return pl.ds(pl.multiple_of(index * width, width), width)


def remote(src, dst, sems, at, peer, there=None):
    return pltpu.make_async_remote_copy(src_ref=src, dst_ref=dst, send_sem=sems[0].at[at],
                                        recv_sem=sems[1].at[at if there is None else there],
                                        device_id=peer, device_id_type=pl.DeviceIdType.MESH)


def arrived(ref, sem):
    pltpu.make_async_copy(ref, ref, sem).wait()


def kernel(q, g, o, k, v, xin, dqo, dko, dvo, wo,
           kv, kt, qr, gr, dr, xl, dl, qn, gn, rs, sh, S, E, dka, dva, dqt, partk, partv, rcvk, rcvv, fink, finv,
           xp, xr, xt, dvall, wrc, wrp, w3, wrh, *sems):
    (lg, lo), sk, sv, sq, sg, sd, sx, sb, sc, sc2, sdq, spk, spv, srk, srv, sdv, swc, swp, swh = [
        sems[i:i + 2] for i in range(0, 38, 2)]
    x, z, y, h, c = (lax.axis_index(a) for a in ("x", "z", "y", "h", "c"))
    me = 8 * x + 4 * z + y

    def mod4(i):
        return lax.rem(i + 4, 4)

    xs = [mod4(x + d) for d in range(4)]
    ys = [mod4(y + e) for e in range(4)]
    hs = [mod4(h + e) for e in range(4)]
    near = [(dz, e) for dz in range(2) for e in range(4) if dz or e]

    def in_plane(dz, e):
        return {"z": (1 - z) if dz else z, "y": ys[e]}

    def in_side(dz, d):
        return {"x": xs[d], "z": (1 - z) if dz else z}

    barrier = pltpu.get_barrier_semaphore()
    friends = [{"x": xs[d], "y": ys[e]} for d in range(4) for e in range(4) if d or e]
    friends += [in_plane(1, e) for e in range(4)] + [in_side(1, d) for d in (1, 2, 3)]
    friends += [{"c": 1 - c}] + [{"h": hs[e]} for e in (1, 2, 3)]
    for friend in friends:
        pl.semaphore_signal(barrier, inc=1, device_id=friend, device_id_type=pl.DeviceIdType.MESH)
    get_g = [pltpu.make_async_copy(g.at[0, :, cols(j, LANES)], xp.at[j, :, 0:LANES], lg.at[j]) for j in range(4)]
    get_o = pltpu.make_async_copy(o.at[0], xl.at[:, 0:4 * LANES], lo)
    get_x = pltpu.make_async_copy(xin.at[0], xl, lo)
    for copy in get_g:
        copy.start()
    get_o.start()
    pl.semaphore_wait(barrier, len(friends))

    sends = []

    def send(*a):
        copy = remote(*a)
        copy.start()
        sends.append(copy)

    def spread(src, dst, s, width, which):
        for d in which:
            send(src.at[0, :, cols(xs[d], width)], dst, s, d, {"x": xs[d]})

    def stay(src, dst, s, width):
        pltpu.make_async_copy(src.at[0, :, cols(x, width)], dst, s[1].at[0]).start()

    spread(k, kv.at[me, :, 0:D], sk, D, (1, 3, 2))
    spread(v, kv.at[me, :, D:2 * D], sv, D, (1, 3, 2))
    stay(k, kv.at[me, :, 0:D], sk, D)
    stay(v, kv.at[me, :, D:2 * D], sv, D)
    spread(q, qr.at[x], sq, LANES, (1, 3, 2))
    stay(q, qr.at[x], sq, LANES)
    stay(g, gr.at[x], sg, LANES)

    for copy in get_g:
        copy.wait()
    get_o.wait()
    head = lax.broadcasted_iota(jnp.int32, (HEADS, LANES), 0)
    ones = jnp.where(head == lax.broadcasted_iota(jnp.int32, (HEADS, LANES), 1) // D, 1.0, 0.0).astype(bf)
    for j in range(4):
        at = slice(j * LANES, (j + 1) * LANES)
        prod = xp[j, :, 0:LANES].astype(f32) * xl[:, at].astype(f32)
        high = prod.astype(bf)
        low = (prod - high.astype(f32)).astype(bf)
        dl[j] = dot(ones, high, 1, 1) + dot(ones, low, 1, 1)
    get_x.start()
    for d in (1, 3, 2):
        send(dl.at[xs[d]], dr.at[x], sd, d, {"x": xs[d]})
    pltpu.make_async_copy(dl.at[x], dr.at[x], sd[1].at[0]).start()

    def slot(s, zz, yy):
        return kv.at[8 * s + 4 * zz + yy]

    for s in range(4):
        d = mod4(x - s)
        mine = slot(s, z, y)
        arrived(mine.at[:, 0:D], sk[1].at[d])
        arrived(mine.at[:, D:2 * D], sv[1].at[d])
        send(mine, mine, sb, (s, 0), {"z": 1 - z})
        for e in (1, 3, 2):
            send(mine, mine, sc, (s, e), {"y": ys[e]})

    get_x.wait()
    for j in range(4):
        xp[j] = jnp.concatenate([xl[:, 640 * b + 160 * j:640 * b + 160 * j + 160] for b in range(8)], axis=1)
    dka[...] = jnp.zeros_like(dka)
    dqt[...] = jnp.zeros_like(dqt)

    for s in (0, 1):
        theirs = slot(s + 2, 1 - z, y)
        arrived(theirs, sb[1].at[s + 2, 0])
        for e in (1, 3, 2):
            send(theirs, theirs, sc2, (s + 2, e), {"y": ys[e]})
        for e in (1, 3, 2):
            theirs = slot(s, z, mod4(y - e))
            arrived(theirs, sc[1].at[s, e])
            send(theirs, theirs, sb, (s, e), {"z": 1 - z})
    spread(g, gr.at[x], sg, LANES, (1, 3, 2))
    for e in (1, 3, 2):
        remote(xp.at[ys[e]], xr.at[y], sx, e, {"y": ys[e]}).start()
    pltpu.make_async_copy(xp.at[y], xr.at[y], sx[1].at[0]).start()

    def chunk_of(ch):
        return pl.ds(ch * BLOCKS, BLOCKS)

    def stats(s, carry):
        d = mod4(x - s)
        i = 8 * s + 4 * z + y

        @pl.when(s < 2)
        def _():
            for e in range(4):
                arrived(slot(s, 1 - z, mod4(y - e)), sb[1].at[s, e])

        @pl.when(s >= 2)
        def _():
            for e in (1, 2, 3):
                arrived(slot(s, z, mod4(y - e)), sc[1].at[s, e])
                arrived(slot(s, 1 - z, mod4(y - e)), sc2[1].at[s, e])

        for b in range(8):
            kt[:, cols(8 * s + b, D)] = kv[8 * s + b, :, 0:D].T
        arrived(qr.at[s], sq[1].at[d])
        arrived(dr.at[s], sd[1].at[d])
        for n in range(HEADS):
            cs = slice(n * D, (n + 1) * D)
            qn[s, cs, :] = qr[s, :, cs]
        n = 2 * s + z

        def half(side, carry):
            lanes = cols(side, HALF)

            def rows_of(ch, count, first=0):
                return pl.ds(pl.multiple_of((first + ch) * CHUNK, CHUNK), count * CHUNK)

            def score(ch, count):
                keys = kv[pl.ds(ch * BLOCKS, count * BLOCKS), :, 0:D].reshape(count * CHUNK, D)
                return dot(keys, qn[s, lanes, :], 1, 1)

            def top(m, t):
                return jnp.maximum(m, jnp.max(t.reshape(-1, 8, HALF), axis=0))

            def p1(ch, m, count):
                t = score(ch, count)
                S[rows_of(ch, count), :] = t
                return top(m, t)

            m = lax.fori_loop(0, s, lambda p, m: p1(2 * p, m, 2), jnp.full((8, HALF), -1e30, f32))
            m = lax.fori_loop(2 * s, n, lambda ch, m: p1(ch, m, 1), m)
            last = score(n, 1)
            key = n * CHUNK + lax.broadcasted_iota(jnp.int32, (CHUNK, 1), 0)
            row = i * ROWS + lax.broadcasted_iota(jnp.int32, (1, HALF), 1) % ROWS
            last = jnp.where(key <= row, last, -1e30)
            S[rows_of(n, 1), :] = last
            mc = jnp.max(top(m, last), axis=0, keepdims=True) * LOG

            def p2(ch, total, count):
                e = jnp.exp2(S[rows_of(ch, count), :] * LOG - mc)
                E[rows_of(ch, count, s * (s + 1)), lanes] = e.astype(bf)
                return total + jnp.sum(e.reshape(-1, 8, HALF), axis=0)

            total = lax.fori_loop(0, s, lambda p, t: p2(2 * p, t, 2), jnp.zeros((8, HALF), f32))
            total = lax.fori_loop(2 * s, n + 1, lambda ch, t: p2(ch, t, 1), total)
            rs[s, :, lanes] = 1.0 / jnp.sum(total, axis=0, keepdims=True)
            return carry

        lax.fori_loop(0, 2, half, 0)
        sh[s] = jnp.concatenate([dr[s, a:a + 1, :] for a in range(HEADS)], axis=1) * rs[s]
        return carry

    def scale(s, carry):
        arrived(gr.at[s], sg[1].at[mod4(x - s)])
        heads = jnp.concatenate([rs[s, :, n * D:(n + 1) * D] for n in range(HEADS)], axis=0).T
        for n in range(HEADS):
            cs = slice(n * D, (n + 1) * D)
            gn[s, cs, :] = (gr[s, :, cs].astype(f32) * heads[:, n:n + 1]).astype(bf)
        return carry

    def grads(s, ch, e32):
        at = cols(ch, CHUNK)
        values = kv[chunk_of(ch), :, D:2 * D].reshape(CHUNK, D)
        ds = (e32 * (dot(values, gn[s], 1, 1) - sh[s])).astype(bf)
        dka[at, :] += dot(ds, qn[s], 1, 0)
        dqt[s] += dot(kt[:, at], ds, 1, 0)

    def narrow(s, first, end):
        def one(ch, carry):
            grads(s, ch, E[cols(s * (s + 1) + ch, CHUNK), :].astype(f32))
            return carry

        lax.fori_loop(first, end, one, 0)

    def give_dq(s):
        for n in range(HEADS):
            cs = slice(n * D, (n + 1) * D)
            xl[:, cols(s * HEADS + n, D)] = (dqt[s, :, cs] * SCALE).astype(bf).T
        home = dqo.at[0, :, cols(x, LANES)]

        @pl.when(s == x)
        def _():
            pltpu.make_async_copy(xl.at[:, cols(s, LANES)], home, sdq[1].at[0]).start()

        @pl.when(s != x)
        def _():
            remote(xl.at[:, cols(s, LANES)], home, sdq, mod4(s - x), {"x": s}).start()

    def total_of(part, rcv, sems, s):
        def add(n, total):
            arrived(rcv.at[n, s], sems[1].at[n, s])
            return total + rcv[n, s].astype(f32)

        return lax.fori_loop(1, 8, add, part[s, 4 * z + y].astype(f32)).astype(bf)

    def deliver(src, dst, s2, at, there, s):
        @pl.when(s == x)
        def _():
            pltpu.make_async_copy(src, dst, s2[1].at[there]).start()

        @pl.when(s != x)
        def _():
            remote(src, dst, s2, at, {"x": s}, there).start()

    def reduce_v(s):
        finv[s] = total_of(partv, rcvv, spv, s)
        place = dvall.at[y, :, cols(x, D)]
        for e in (1, 3, 2):
            remote(finv.at[s], place, sdv, (s, e), {"x": s, "y": ys[e]}, (x, y)).start()
        deliver(finv.at[s], place, sdv, (s, 0), (x, y), s)
        deliver(finv.at[s], dvo.at[0, :, cols(x, D)], srv, s, x, s)

    def reduce_k(s):
        fink[s] = total_of(partk, rcvk, spk, s)
        deliver(fink.at[s], dko.at[0, :, cols(x, D)], srk, s, x, s)

    def hand_out(part, rcv, sems, a):
        def one(n, carry):
            to = {"z": lax.rem(z + n // 4, 2), "y": lax.rem(y + n, 4)}
            remote(part.at[a, 4 * to["z"] + to["y"]], rcv.at[n, a], sems, (n, a), to).start()
            return carry

        lax.fori_loop(1, 8, one, 0)

    def values_of(t, carry):
        a = 3 - t

        def share(s, ch, count):
            e = E[pl.ds(pl.multiple_of((s * (s + 1) + ch) * CHUNK, CHUNK), count * CHUNK), :]
            return dot(e, gn[s], 1, 0)

        dva[...] = jnp.zeros_like(dva)

        def both(s, carry):
            dva[...] += share(s, 2 * a, 2)
            return carry

        def one(zz, carry):
            dva[cols(zz, CHUNK), :] += share(a, 2 * a + zz, 1)
            return carry

        lax.fori_loop(a + 1, 4, both, 0)
        lax.fori_loop(0, 1 + z, one, 0)
        for b in range(8):
            partv[a, b] = dva[b * ROWS:(b + 1) * ROWS, :].astype(bf)
        hand_out(partv, rcvv, spv, a)
        return carry

    order = [(1, 2), (1, 1), (1, 3), (0, 2), (0, 1), (0, 3), (1, 0), (0, 0)]

    def piece(dz, d):
        peer = in_side(dz, d)
        return peer, 2 * peer["x"] + peer["z"]

    def turn_x():
        line = lax.broadcasted_iota(jnp.int32, (320, 640), 0)
        want = line + 20 * lax.shift_right_logical(line * 3277, 16)
        place = lax.broadcasted_iota(jnp.int32, (320, 640), 1)
        for e in range(4):
            arrived(xr.at[mod4(y - e)], sx[1].at[e])
        def turn(n, carry):
            part_c, half, j = n // 8, n // 4 % 2, n % 4
            pick = jnp.where(place == want + 20 * part_c, 1.0, 0.0).astype(bf)
            rows = dot(pick, xr[j, :, cols(half, 640)], 1, 1).astype(bf)
            xt[part_c, pl.ds(half * 4, 4), :, cols(j, ROWS)] = rows.reshape(4, 80, ROWS)
            return carry

        lax.fori_loop(0, 16, turn, 0)

    def weigh():
        def wait(n, carry):
            arrived(dvall.at[n % 4, :, cols(n // 4, D)], sdv[1].at[n // 4, n % 4])
            return carry

        lax.fori_loop(0, 16, wait, 0)
        tall = dvall[...].reshape(4 * ROWS, 4 * D)

        def product(half, carry):
            xt[half] = dot(xt[half].reshape(640, 4 * ROWS), tall, 1, 0).astype(bf).reshape(8, 80, 4 * D)
            return carry

        lax.fori_loop(0, 2, product, 0)
        for n, (dz, d) in enumerate(order):
            b = piece(dz, d)[1]
            remote(xt.at[1 - c, b], wrc.at[b], swc, n, {"c": 1 - c}).start()

    def over_sides():
        for n, (dz, d) in enumerate(order):
            peer, b = piece(dz, d)
            arrived(wrc.at[b], swc[1].at[n])
            wrc[b] = (xt[c, b].astype(f32) + wrc[b].astype(f32)).astype(bf)
            if dz or d:
                remote(wrc.at[b], wrp.at[dz * 4 + d], swp, dz * 4 + d, peer).start()

    def over_rest():
        total = wrc[2 * x + z].astype(f32)
        for dz, d in near:
            n = dz * 4 + d
            arrived(wrp.at[n], swp[1].at[n])
            total = total + wrp[n].astype(f32)
        for e in range(4):
            w3[e] = jnp.concatenate([total[20 * e:20 * e + 20], jnp.zeros((12, 4 * D), f32)], axis=0).astype(bf)
        for e in (1, 3, 2):
            remote(w3.at[hs[e]], wrh.at[e], swh, e, {"h": hs[e]}).start()

    def give_two(first):
        lax.fori_loop(first, first + 2, lambda s, carry: (give_dq(s), carry)[1], 0)

    def step(t, carry):
        early = 1 - jnp.minimum(t // 2, 1)
        a = (1 - early) * (3 - (t - 2) // 2)
        s = early * t + (1 - early) * (3 - t % 2)
        narrow(s, 2 * a, jnp.minimum(2 * a + 2 + 2 * early, 2 * s + 1 + z))

        @pl.when(t == 0)
        def _():
            turn_x()
            lax.fori_loop(0, 4, lambda n, carry: (reduce_v(3 - n), carry)[1], 0)

        @pl.when(jnp.logical_and(t > 1, t % 2 == 1))
        def _():
            def one(b, carry):
                partk[a, b] = (dka[cols(8 * a + b, ROWS), :] * SCALE).astype(bf)
                return carry

            lax.fori_loop(0, 8, one, 0)
            hand_out(partk, rcvk, spk, a)

        @pl.when(jnp.logical_and(t > 4, t % 2 == 1))
        def _():
            reduce_k(a + 1)


        pl.when(t == 1)(weigh)
        pl.when(t == 3)(over_sides)
        pl.when(t == 3)(lambda: give_two(0))
        pl.when(t == 7)(over_rest)
        return carry

    lax.fori_loop(0, 4, stats, 0)
    lax.fori_loop(0, 4, scale, 0)
    lax.fori_loop(0, 4, values_of, 0)
    lax.fori_loop(0, 10, step, 0)
    give_two(2)
    last = w3[h].astype(f32)
    for e in (1, 3, 2):
        arrived(wrh.at[e], swh[1].at[e])
        last = last + wrh[e].astype(f32)
    wo[...] = last[0:20]
    reduce_k(0)

    for d in range(4):
        f = mod4(x - d)
        arrived(dqo.at[0, :, cols(f, LANES)], sdq[1].at[d])
        arrived(dko.at[0, :, cols(d, D)], srk[1].at[d])
        arrived(dvo.at[0, :, cols(d, D)], srv[1].at[d])
    for copy in sends:
        copy.wait_send()
    for e in (1, 2, 3):
        remote(xp.at[ys[e]], xr.at[y], sx, e, {"y": ys[e]}).wait_send()
    for d in (1, 2, 3):
        remote(xl.at[:, cols(xs[d], LANES)], dqo.at[0, :, cols(x, LANES)], sdq, d, {"x": xs[d]}).wait_send()
    def sent(n, carry):
        to = {"z": lax.rem(z + n // 4, 2), "y": lax.rem(y + n, 4)}
        for a in range(4):
            remote(partk.at[a, 0], rcvk.at[n, a], spk, (n, a), to).wait_send()
            remote(partv.at[a, 0], rcvv.at[n, a], spv, (n, a), to).wait_send()
        return carry

    lax.fori_loop(1, 8, sent, 0)
    for s in range(4):
        for e in (1, 2, 3):
            remote(finv.at[s], dvall.at[y, :, cols(x, D)], sdv, (s, e), {"y": ys[e]}).wait_send()
    for d in (1, 2, 3):
        t = xs[d]
        remote(finv.at[t], dvall.at[y, :, cols(x, D)], sdv, (t, 0), {"x": t}).wait_send()
        remote(fink.at[t], dko.at[0, :, cols(x, D)], srk, t, {"x": t}).wait_send()
        remote(finv.at[t], dvo.at[0, :, cols(x, D)], srv, t, {"x": t}).wait_send()
    for n, (dz, d) in enumerate(order):
        peer, b = piece(dz, d)
        remote(xt.at[1 - c, b], wrc.at[b], swc, n, {"c": 1 - c}).wait_send()
        if dz or d:
            remote(wrc.at[b], wrp.at[dz * 4 + d], swp, dz * 4 + d, peer).wait_send()
    for e in (1, 2, 3):
        remote(w3.at[hs[e]], wrh.at[e], swh, e, {"h": hs[e]}).wait_send()


def per_device(x_in, q, k, v, o, g):
    T = 32 * ROWS
    anyspace = pl.BlockSpec(memory_space=pl.ANY)
    sems = [(4,), ()] + [(4,)] * 12 + [(4, 4)] * 6 + [(4,)] * 2 + [(8, 4)] * 4 + [(4,)] * 4 + [(4, 4)] * 2 + [(8,)] * 2
    sems += [(8,)] * 2 + [(4,)] * 2
    tall = (T, D)
    scratch = [((32, ROWS, 2 * D), bf), ((D, T), bf), ((4, ROWS, LANES), bf), ((4, ROWS, LANES), bf), ((4, HEADS, ROWS), f32),
               ((ROWS, 4 * XCOLS), bf), ((4, HEADS, ROWS), f32),
               ((4, LANES, D), bf), ((4, LANES, D), bf), ((4, 1, LANES), f32), ((4, 1, LANES), f32),
               ((T, HALF), f32), ((20 * CHUNK, LANES), bf), (tall, f32), ((2 * CHUNK, D), f32), ((4, D, LANES), f32),
               ((4, 8, ROWS, D), bf), ((4, 8, ROWS, D), bf), ((8, 4, ROWS, D), bf),
               ((8, 4, ROWS, D), bf), ((4, ROWS, D), bf), ((4, ROWS, D), bf),
               ((4, ROWS, XCOLS), bf), ((4, ROWS, XCOLS), bf), ((2, 8, 80, 4 * ROWS), bf), ((4, ROWS, 4 * D), bf),
               ((8, 80, 4 * D), bf), ((8, 80, 4 * D), bf),
               ((4, 32, 4 * D), bf), ((4, 32, 4 * D), bf)]
    return pl.pallas_call(
        kernel,
        out_shape=[jax.ShapeDtypeStruct((1, ROWS, 4 * LANES), bf), jax.ShapeDtypeStruct((1, ROWS, 4 * D), bf),
                   jax.ShapeDtypeStruct((1, ROWS, 4 * D), bf), jax.ShapeDtypeStruct((20, 4 * D), f32)],
        in_specs=[anyspace] * 6,
        out_specs=[anyspace] * 3 + [pl.BlockSpec(memory_space=pltpu.VMEM)],
        scratch_shapes=[pltpu.VMEM(*s) for s in scratch] + [pltpu.SemaphoreType.DMA(s) for s in sems],
        compiler_params=pltpu.CompilerParams(vmem_limit_bytes=60 << 20, collective_id=0, has_side_effects=True),
        name="attention_backward")(q, g, o, k, v, x_in)


def solution(mesh):
    fine = Mesh(mesh.devices.reshape(4, 2, 4, 4, 2), ("x", "z", "y", "h", "c"))
    seq, dp = ("x", "z", "y"), ("h", "c")
    rows = P(dp, seq, None)
    return jax.shard_map(per_device, mesh=fine, in_specs=(rows,) * 6,
                         out_specs=(rows, rows, rows, P(seq + dp, None)), check_vma=False)
```

time: 119 us -> 108 us (0.908)
  Pallas kernels: 114 us -> 103 us
    pallas_call x1, Pallas kernels: 114 us -> 103 us  [per_device(): pl.pallas_call(kernel, out_shape=[jax.ShapeDtypeStruct((1, ROWS, 4 * LANE...]
where the time goes in v5:
time: 108 us
  Pallas kernels  103 us (95%)
  local copies, waits for them, and re-layouts  4.27 us (4%)
    pallas_call x1, Pallas kernels, per_device(): pl.pallas_call(kernel, out_shape=[jax.ShapeDtypeStruct((1, ROWS, 4 * LANE...  103 us
    unnamed x10, local copies, waits for them, and re-layouts  4.27 us

profile of v5, /device:TPU:6, one launch (start us, length us, event | category | flops | bytes accessed | tf_op | source)
XLA Modules:
  0.0 108.2 jit_solution(2543137875537675547)
XLA Ops:
  0.6 103.3 %attention_backward.1 = (bf16[1,128,4096]{2,1,0:T(8,128)(2,1)}, bf16[1,128,512]{2,1,0:T(8,128)(2,1)}, bf16[1,128,512]{2,1,0:T(8,128)(2,1)}, f32[20,512]{1,0:T(8,128)}) custom-call(bf16[1,128,4096]{2,1,0:T(8,128)(2,1)} %q.1, bf16[1,128,4096]{2,1,0:T(8,128)(2,1)} %g.1, bf16[1,128,4096]{2,1,0:T(8,128)(2,1)} %o.1, bf16[1,128,512]{2,1,0:T(8,128)(2,1)} %k.1, ...), custom_call_target="tpu_custom_call" | custom-call | tf_op jit(solution)/shard_map/attention_backward/pallas_call | solution.py:464
  103.9 0.0 copy-start.1
  104.0 0.0 copy-start
  104.0 0.0 copy-start.2
  104.0 2.3 %copy.14 = bf16[1,128,4096]{2,1,0:T(8,128)(2,1)} copy(bf16[1,128,4096]{2,1,0:T(8,128)(2,1)} %get-tuple-element.8) | data formatting | bytes 2097152
  106.3 0.0 copy-done.1
  106.3 0.7 copy.15
  107.0 0.0 copy-done
  107.0 0.7 copy.16
  107.6 0.0 copy-done.2
  107.6 0.6 copy.17
Async XLA Ops:
  103.9 2.4 %copy-start.1 = (bf16[1,128,512]{2,1,0:T(8,128)(2,1)S(1)}, bf16[1,128,512]{2,1,0:T(8,128)(2,1)}, u32[]{:S(2)}) copy-start(bf16[1,128,512]{2,1,0:T(8,128)(2,1)} %get-tuple-element.9) | copy-start | bytes 393220
  104.0 3.0 %copy-start = (bf16[1,128,512]{2,1,0:T(8,128)(2,1)S(1)}, bf16[1,128,512]{2,1,0:T(8,128)(2,1)}, u32[]{:S(2)}) copy-start(bf16[1,128,512]{2,1,0:T(8,128)(2,1)} %get-tuple-element.10) | copy-start | bytes 393220
  104.0 3.7 %copy-start.2 = (f32[20,512]{1,0:T(8,128)S(1)}, f32[20,512]{1,0:T(8,128)}, u32[]{:S(2)}) copy-start(f32[20,512]{1,0:T(8,128)} %get-tuple-element.11) | copy-start | bytes 122884

commit v6 on v5

--- a/solution.py
+++ b/solution.py
@@ -375,7 +375,6 @@
 
         @pl.when(t == 0)
         def _():
-            turn_x()
             lax.fori_loop(0, 4, lambda n, carry: (reduce_v(3 - n), carry)[1], 0)
 
         @pl.when(jnp.logical_and(t > 1, t % 2 == 1))
@@ -395,20 +394,21 @@
         pl.when(t == 1)(weigh)
         pl.when(t == 3)(over_sides)
         pl.when(t == 3)(lambda: give_two(0))
-        pl.when(t == 7)(over_rest)
+        pl.when(t == 8)(over_rest)
         return carry
 
     lax.fori_loop(0, 4, stats, 0)
     lax.fori_loop(0, 4, scale, 0)
     lax.fori_loop(0, 4, values_of, 0)
+    turn_x()
     lax.fori_loop(0, 10, step, 0)
     give_two(2)
+    reduce_k(0)
     last = w3[h].astype(f32)
     for e in (1, 3, 2):
         arrived(wrh.at[e], swh[1].at[e])
         last = last + wrh[e].astype(f32)
     wo[...] = last[0:20]
-    reduce_k(0)
 
     for d in range(4):
         f = mod4(x - d)

time: 108 us -> 108 us (level)
  no operation moved by 1% of the time
where the time goes in v6:
time: 108 us
  Pallas kernels  103 us (95%)
  local copies, waits for them, and re-layouts  4.27 us (4%)
    pallas_call x1, Pallas kernels, per_device(): pl.pallas_call(kernel, out_shape=[jax.ShapeDtypeStruct((1, ROWS, 4 * LANE...  103 us
    unnamed x10, local copies, waits for them, and re-layouts  4.27 us

profile of v6, /device:TPU:6, one launch (start us, length us, event | category | flops | bytes accessed | tf_op | source)
XLA Modules:
  0.0 107.6 jit_solution(10617181794985873972)
XLA Ops:
  0.6 102.7 %attention_backward.1 = (bf16[1,128,4096]{2,1,0:T(8,128)(2,1)}, bf16[1,128,512]{2,1,0:T(8,128)(2,1)}, bf16[1,128,512]{2,1,0:T(8,128)(2,1)}, f32[20,512]{1,0:T(8,128)}) custom-call(bf16[1,128,4096]{2,1,0:T(8,128)(2,1)} %q.1, bf16[1,128,4096]{2,1,0:T(8,128)(2,1)} %g.1, bf16[1,128,4096]{2,1,0:T(8,128)(2,1)} %o.1, bf16[1,128,512]{2,1,0:T(8,128)(2,1)} %k.1, ...), custom_call_target="tpu_custom_call" | custom-call | tf_op jit(solution)/shard_map/attention_backward/pallas_call | solution.py:464
  103.3 0.0 copy-start.1
  103.3 0.0 copy-start
  103.4 0.0 copy-start.2
  103.4 2.3 %copy.14 = bf16[1,128,4096]{2,1,0:T(8,128)(2,1)} copy(bf16[1,128,4096]{2,1,0:T(8,128)(2,1)} %get-tuple-element.8) | data formatting | bytes 2097152
  105.7 0.0 copy-done.1
  105.7 0.7 copy.15
  106.4 0.0 copy-done
  106.4 0.7 copy.16
  107.0 0.0 copy-done.2
  107.0 0.6 copy.17
Async XLA Ops:
  103.3 2.4 %copy-start.1 = (bf16[1,128,512]{2,1,0:T(8,128)(2,1)S(1)}, bf16[1,128,512]{2,1,0:T(8,128)(2,1)}, u32[]{:S(2)}) copy-start(bf16[1,128,512]{2,1,0:T(8,128)(2,1)} %get-tuple-element.9) | copy-start | bytes 393220
  103.3 3.0 %copy-start = (bf16[1,128,512]{2,1,0:T(8,128)(2,1)S(1)}, bf16[1,128,512]{2,1,0:T(8,128)(2,1)}, u32[]{:S(2)}) copy-start(bf16[1,128,512]{2,1,0:T(8,128)(2,1)} %get-tuple-element.10) | copy-start | bytes 393220
  103.4 3.7 %copy-start.2 = (f32[20,512]{1,0:T(8,128)S(1)}, f32[20,512]{1,0:T(8,128)}, u32[]{:S(2)}) copy-start(f32[20,512]{1,0:T(8,128)} %get-tuple-element.11) | copy-start | bytes 122884

commit v7 on v6

--- a/solution.py
+++ b/solution.py
@@ -269,7 +269,6 @@
         for e in (1, 3, 2):
             remote(finv.at[s], place, sdv, (s, e), {"x": s, "y": ys[e]}, (x, y)).start()
         deliver(finv.at[s], place, sdv, (s, 0), (x, y), s)
-        deliver(finv.at[s], dvo.at[0, :, cols(x, D)], srv, s, x, s)
 
     def reduce_k(s):
         fink[s] = total_of(partk, rcvk, spk, s)
@@ -336,14 +335,19 @@
         lax.fori_loop(0, 16, wait, 0)
         tall = dvall[...].reshape(4 * ROWS, 4 * D)
 
-        def product(half, carry):
+        def product(n, carry):
+            half = (1 - c) + n * (2 * c - 1)
             xt[half] = dot(xt[half].reshape(640, 4 * ROWS), tall, 1, 0).astype(bf).reshape(8, 80, 4 * D)
+
+            @pl.when(n == 0)
+            def _():
+                for m, (dz, d) in enumerate(order):
+                    b = piece(dz, d)[1]
+                    remote(xt.at[1 - c, b], wrc.at[b], swc, m, {"c": 1 - c}).start()
+
             return carry
 
         lax.fori_loop(0, 2, product, 0)
-        for n, (dz, d) in enumerate(order):
-            b = piece(dz, d)[1]
-            remote(xt.at[1 - c, b], wrc.at[b], swc, n, {"c": 1 - c}).start()
 
     def over_sides():
         for n, (dz, d) in enumerate(order):
@@ -367,6 +371,14 @@
     def give_two(first):
         lax.fori_loop(first, first + 2, lambda s, carry: (give_dq(s), carry)[1], 0)
 
+    def give_early():
+        def one(s, carry):
+            deliver(finv.at[s], dvo.at[0, :, cols(x, D)], srv, s, x, s)
+            return carry
+
+        lax.fori_loop(0, 4, one, 0)
+        give_two(0)
+
     def step(t, carry):
         early = 1 - jnp.minimum(t // 2, 1)
         a = (1 - early) * (3 - (t - 2) // 2)
@@ -393,7 +405,7 @@
 
         pl.when(t == 1)(weigh)
         pl.when(t == 3)(over_sides)
-        pl.when(t == 3)(lambda: give_two(0))
+        pl.when(t == 3)(give_early)
         pl.when(t == 8)(over_rest)
         return carry
 

time: 108 us -> 107 us (level)
    pallas_call x1, Pallas kernels: 103 us -> 102 us  [per_device(): pl.pallas_call(kernel, out_shape=[jax.ShapeDtypeStruct((1, ROWS, 4 * LANE...]
where the time goes in v7:
time: 107 us; the launch traced here: 106 us
  Pallas kernels  102 us (95%)
  local copies, waits for them, and re-layouts  4.27 us (4%)
    pallas_call x1, Pallas kernels, per_device(): pl.pallas_call(kernel, out_shape=[jax.ShapeDtypeStruct((1, ROWS, 4 * LANE...  102 us
    unnamed x10, local copies, waits for them, and re-layouts  4.27 us

profile of v7, /device:TPU:6, one launch (start us, length us, event | category | flops | bytes accessed | tf_op | source)
XLA Modules:
  0.0 106.5 jit_solution(9025597342873148005)
XLA Ops:
  0.6 101.5 %attention_backward.1 = (bf16[1,128,4096]{2,1,0:T(8,128)(2,1)}, bf16[1,128,512]{2,1,0:T(8,128)(2,1)}, bf16[1,128,512]{2,1,0:T(8,128)(2,1)}, f32[20,512]{1,0:T(8,128)}) custom-call(bf16[1,128,4096]{2,1,0:T(8,128)(2,1)} %q.1, bf16[1,128,4096]{2,1,0:T(8,128)(2,1)} %g.1, bf16[1,128,4096]{2,1,0:T(8,128)(2,1)} %o.1, bf16[1,128,512]{2,1,0:T(8,128)(2,1)} %k.1, ...), custom_call_target="tpu_custom_call" | custom-call | tf_op jit(solution)/shard_map/attention_backward/pallas_call | solution.py:476
  102.2 0.0 copy-start.1
  102.2 0.0 copy-start
  102.2 0.0 copy-start.2
  102.2 2.3 %copy.14 = bf16[1,128,4096]{2,1,0:T(8,128)(2,1)} copy(bf16[1,128,4096]{2,1,0:T(8,128)(2,1)} %get-tuple-element.8) | data formatting | bytes 2097152
  104.5 0.0 copy-done.1
  104.5 0.7 copy.15
  105.2 0.0 copy-done
  105.2 0.7 copy.16
  105.9 0.0 copy-done.2
  105.9 0.6 copy.17
Async XLA Ops:
  102.2 2.4 %copy-start.1 = (bf16[1,128,512]{2,1,0:T(8,128)(2,1)S(1)}, bf16[1,128,512]{2,1,0:T(8,128)(2,1)}, u32[]{:S(2)}) copy-start(bf16[1,128,512]{2,1,0:T(8,128)(2,1)} %get-tuple-element.9) | copy-start | bytes 393220
  102.2 3.0 %copy-start = (bf16[1,128,512]{2,1,0:T(8,128)(2,1)S(1)}, bf16[1,128,512]{2,1,0:T(8,128)(2,1)}, u32[]{:S(2)}) copy-start(bf16[1,128,512]{2,1,0:T(8,128)(2,1)} %get-tuple-element.10) | copy-start | bytes 393220
  102.2 3.7 %copy-start.2 = (f32[20,512]{1,0:T(8,128)S(1)}, f32[20,512]{1,0:T(8,128)}, u32[]{:S(2)}) copy-start(f32[20,512]{1,0:T(8,128)} %get-tuple-element.11) | copy-start | bytes 122884
